TPU v7x, 32 devices: a whole 2x2x4 slice. The times are simulated.
32 devices in a mesh: grp: 4 (over x, core), dev: 8 (over z, y).
Axes of the slice: x: 2, y: 2, z: 4, core: 2. Of those that a mesh axis runs over, the one named last changes fastest.
Arguments:
- parent_state: float32 [24, 256, 1024], P(None, 'grp', 'dev'), may hold values from -6 to 6
- nest_state: float32 [8, 24, 192, 384], P('grp', None, 'dev'), may hold values from -6 to 6
- nest_anchor: int32 [8, 2], replicated, may hold values from 0 to 896, as said below
- diffusion: float32 [2, 24], replicated, may hold values from 0.02 to 0.05
- courant: float32 [2, 24], replicated, may hold values from 0.05 to 0.15
Outputs:
- parent_out: float32 [24, 256, 1024], P(None, 'grp', 'dev')
- nest_out: float32 [8, 24, 192, 384], P('grp', None, 'dev')
Inputs may be any that keep to these rules, and one draw needn't show every extreme that they name: `nest_anchor`: the parent grid is cut into 2 x 8 / 2 disjoint bands of 128 x 256 cells; each nest lies in a band of its own, its 64 x 128 covered cells inside that band.
All inputs are finite; a program needn't handle non-finite values.
Results may differ from a plain program's by a relative error of at most 0.0003.
Values sent between devices are 32-bit elements; how exact they have to be, the bound alone decides.
No kernel may reach another device: no remote copies, remote signals or barrier semaphores. Data moves between devices by JAX's collectives and lax.ppermute only.
A program may use at most 320 MiB of HBM per device.

v0:
```python
import functools

import jax
import jax.numpy as jnp
from jax import lax
from jax.experimental import pallas as pl
from jax.experimental.pallas import tpu as pltpu
from jax.sharding import PartitionSpec as P

F32 = jnp.float32
BF16 = jnp.bfloat16
LANES = 128
VMEM_LIMIT = 63 * 1024 * 1024
MID, EAST, WEST, NORTH, SOUTH = range(5)


class Sizes:
    def __init__(self, parent, nest, anchor, grp_count, dev_count):
        self.C, self.TR, self.TC = parent.shape
        self.L, _, self.H, self.W = nest.shape
        self.N = anchor.shape[0]
        self.G, self.D = grp_count, dev_count
        self.M = self.H // 3
        self.FR, self.FC = self.M * self.D, self.W // 3
        self.S = self.G // 2
        self.NB = self.N // 2
        self.Y = self.D // self.NB
        self.CS = self.C // self.S
        self.BR, self.BC = self.S * self.TR, self.Y * self.TC
        self.R1 = self.L * self.CS * (self.M + 2)
        self.R2 = self.CS * (self.M + 2)
        self.RING = self.FR + self.L * 2 * self.C
        self.RG = self.RING + self.C
        self.RG2 = 16 + self.L * self.C + 8
        self.HALO = self.L * self.C * 3
        self.EDGE = 3 * self.HALO
        assert self.H == 24 and self.FC == LANES and self.TC == LANES
        assert self.FR >= self.TR and self.L == 2


def call(body, out_shape, smem, args, scratch=(), raw=(), early=None):
    moved = [*smem, *args]
    n_in, n_raw, n_out = len(moved), len(raw), len(out_shape)
    place = pl.BlockSpec(memory_space=pltpu.HBM)

    def kernel(*refs):
        source, refs = refs[:n_in], refs[n_in:]
        stay, refs = refs[:n_raw], refs[n_raw:]
        target, refs = refs[:n_out], refs[n_out:]
        inner, refs = refs[:n_in], refs[n_in:]
        result, refs = refs[:n_out], refs[n_out:]
        extra, sem = refs[:-1], refs[-1]
        fetch = [pltpu.make_async_copy(a, b, sem.at[k]) for k, (a, b) in enumerate(zip(source, inner))]
        for copy in fetch:
            copy.start()
        for copy in fetch:
            copy.wait()
        store = [
            pltpu.make_async_copy(a, b, sem.at[n_in + k]) for k, (a, b) in enumerate(zip(result, target))
        ]
        if early is None:
            body(*inner, *stay, *result, *extra)
        else:
            body(*inner, *stay, *result, *extra, store[early].start)
        for k, copy in enumerate(store):
            if k != early:
                copy.start()
        for copy in store:
            copy.wait()

    return pl.pallas_call(
        kernel,
        out_shape=list(out_shape),
        in_specs=[place] * (n_in + n_raw),
        out_specs=[place] * n_out,
        scratch_shapes=[
            *[pltpu.SMEM(x.shape, x.dtype) for x in smem],
            *[pltpu.VMEM(x.shape, x.dtype) for x in args],
            *[pltpu.VMEM(x.shape, x.dtype) for x in out_shape],
            *scratch,
            pltpu.SemaphoreType.DMA((n_in + n_out,)),
        ],
        compiler_params=pltpu.CompilerParams(vmem_limit_bytes=VMEM_LIMIT),
    )(*moved, *raw)


def iota(shape, dim):
    return lax.broadcasted_iota(jnp.int32, shape, dim)


def split_dot(x, table):
    high = x.astype(BF16)
    low = (x - high.astype(F32)).astype(BF16)
    return jnp.dot(jnp.concatenate([high, low], axis=1), table, preferred_element_type=F32)


def nest_at(z, anc, band):
    found = 0
    for n in range(z.N):
        found += jnp.where(anc[0, n] // z.BR * z.NB + anc[1, n] // z.BC == band, n, 0)
    return found


def weights(diff, cour, c, times):
    splat = lambda ref, k: jnp.full((8, LANES), ref[k, c], F32)
    east = times * splat(diff, 0)
    north = times * splat(diff, 1)
    west = east + splat(cour, 0)
    south = north + splat(cour, 1)
    return 1.0 - (east + west) - (north + south), east, west, north, south


def ghost_share(inject, back, mid, plus, minus):
    stay = mid + inject
    m0 = inject * (1.0 + stay + mid * stay + inject * (stay + back) + 2.0 * plus * minus)
    p1 = inject * plus * (1.0 + 2.0 * stay)
    p2 = inject * plus * plus
    n1 = inject * minus * (1.0 + 2.0 * stay)
    n2 = inject * minus * minus
    ninth = 1.0 / 9.0
    same = (3.0 * m0 + 2.0 * p1 + p2 + 2.0 * n1 + n2) * ninth
    return same, (p1 + 2.0 * p2) * ninth, (n1 + 2.0 * n2) * ninth, inject * plus * minus * ninth


class Strip:
    def __init__(self):
        sub = iota((8, LANES), 0)
        lane = iota((8, LANES), 1)
        self.high = [sub == 0, sub == 4]
        self.low = [sub == 7, sub == 3]
        self.any_high = (sub == 0) | (sub == 4)
        self.any_low = (sub == 7) | (sub == 3)
        self.first, self.last = lane == 0, lane == LANES - 1

    def east(self, x, ghost):
        return jnp.where(self.last, ghost, pltpu.roll(x, LANES - 1, 1))

    def west(self, x, ghost):
        return jnp.where(self.first, ghost, pltpu.roll(x, 1, 1))

    def north(self, mains, cap):
        up = [pltpu.roll(m, 7, 0) for m in mains]
        cap_up = pltpu.roll(cap, 7, 0)
        new = [jnp.where(self.low[l], cap_up, up[l]) for l in range(2)]
        return new, jnp.where(self.low[0], up[0], jnp.where(self.low[1], up[1], 0.0))

    def south(self, mains, cap):
        down = [pltpu.roll(m, 1, 0) for m in mains]
        cap_down = pltpu.roll(cap, 1, 0)
        new = [jnp.where(self.high[l], cap_down, down[l]) for l in range(2)]
        return new, jnp.where(self.high[0], down[0], jnp.where(self.high[1], down[1], 0.0))

    def step(self, u, co, west_ghost, east_ghost):
        n_in = [self.north([u[0][0][x], u[1][0][x]], u[2][0][x]) for x in range(3)]
        s_in = [self.south([u[0][2][x], u[1][2][x]], u[2][2][x]) for x in range(3)]
        pick = lambda pair, k: pair[1] if k == 2 else pair[0][k]
        new = []
        for k in range(3):
            rows = []
            for y in range(3):
                row = u[k][y]
                e = [row[1], row[2], self.east(row[0], east_ghost[k])]
                w = [self.west(row[2], west_ghost[k]), row[0], row[1]]
                cells = []
                for x in range(3):
                    n = u[k][y + 1][x] if y < 2 else pick(n_in[x], k)
                    s = u[k][y - 1][x] if y > 0 else pick(s_in[x], k)
                    cells.append(
                        co[MID] * row[x]
                        + (co[EAST] * e[x] + co[WEST] * w[x])
                        + (co[NORTH] * n + co[SOUTH] * s)
                    )
                rows.append(cells)
            new.append(rows)
        return new

    def pooled_step(self, u, co):
        ends = []
        for k in range(3):
            row = [u[k][y][0] + u[k][y][1] + u[k][y][2] for y in range(3)]
            col = [u[k][0][x] + u[k][1][x] + u[k][2][x] for x in (0, 2)]
            ends.append((row[0], row[2], col[0], col[1], row[0] + row[1] + row[2]))
        n_in = self.north([ends[0][0], ends[1][0]], ends[2][0])
        s_in = self.south([ends[0][1], ends[1][1]], ends[2][1])
        pick = lambda pair, k: pair[1] if k == 2 else pair[0][k]
        out = []
        for k in range(3):
            row0, row2, col0, col2, total = ends[k]
            flux_x = co[EAST] * (self.east(col0, 0.0) - col0)
            flux_x += co[WEST] * (self.west(col2, 0.0) - col2)
            flux_y = co[NORTH] * (pick(n_in, k) - row0) + co[SOUTH] * (pick(s_in, k) - row2)
            out.append(total + (flux_x + flux_y))
        return out


def phase_rows(z, ref, l, c, y, x):
    got = ref[x, pl.ds((l * z.C + c) * z.H + y, z.M, 3), :]
    return got if l == 0 else pltpu.roll(got, 4, 0)


def partial_averages(z, diff, cour, nest, *refs):
    out, (phases, strips, sem, store_phases) = refs[: z.S], refs[z.S :]
    fetch = [pltpu.make_async_copy(nest.at[l], strips.at[l], sem.at[l]) for l in range(z.L)]
    for copy in fetch:
        copy.start()
    d = lax.axis_index("dev")
    own = lax.rem(lax.axis_index("grp"), z.S)
    C, M, CS = z.C, z.M, z.CS
    fine = lax.rem(iota((2 * z.W, z.W), 0), z.W)
    place = iota((2 * z.W, z.W), 1)
    at = lax.rem(place, LANES) * 3 + place // LANES
    deal = jnp.where(fine == at, 1.0, 0.0).astype(BF16)
    rows = C * z.H
    for l in range(z.L):
        fetch[l].wait()
        dealt = split_dot(strips[l].reshape(rows, z.W), deal)
        for x in range(3):
            phases[x, l * rows : (l + 1) * rows, :] = dealt[:, x * LANES : (x + 1) * LANES]
    store_phases()
    strip = Strip()
    keep_high = strip.any_low | (strip.any_high & (d < z.D - 1))
    keep_low = strip.any_high | (strip.any_low & (d > 0))
    zero = jnp.zeros((8, LANES), F32)
    ghosts = [0.0] * 3
    base = z.L * CS * M

    def hold(u):
        cap = [
            [jnp.where(keep_high, v, 0.0) for v in u[2][0]],
            u[2][1],
            [jnp.where(keep_low, v, 0.0) for v in u[2][2]],
        ]
        return [u[0], u[1], cap]

    for part in range(z.S):

        def channel(i, _, to=out[part], first=jnp.bitwise_xor(own, part) * CS):
            c = first + i
            co = weights(diff, cour, c, 3.0)
            u = [
                [[phase_rows(z, phases, l, c, y, x) for x in range(3)] for y in range(3)]
                for l in range(2)
            ]
            u.append([[zero] * 3] * 3)
            for _step in range(2):
                u = hold(strip.step(u, co, ghosts, ghosts))
            got = [v * (1.0 / 9.0) for v in strip.pooled_step(u, co)]
            got[1] = pltpu.roll(got[1], 4, 0)
            for l in range(2):
                row = pl.multiple_of((l * CS + i) * M, M)
                to[pl.ds(row, M), :] = got[l]
                for side, sub in enumerate(((7, 3), (0, 4))):
                    row = base + (l * 2 + side) * CS + i
                    to[pl.ds(row, 1), :] = got[2][sub[l] : sub[l] + 1]
            return 0

        lax.fori_loop(0, CS, channel, 0, unroll=2)


def pick_band(z, anc, *refs):
    got, out = refs[: z.G], refs[z.G]
    g = lax.axis_index("grp")
    top = g // z.S * z.NB
    base, size = z.L * z.CS * z.M, z.CS * z.M
    for band in range(z.NB):
        n = nest_at(z, anc, top + band)
        of = n // z.L
        slot = jnp.bitwise_xor(of, g)
        first = n - of * z.L == 0
        for k in range(z.G):

            @pl.when(slot == k)
            def _(k=k, first=first, band=band):
                main = jnp.where(first, got[k][:size, :], got[k][size : 2 * size, :])
                edge = jnp.where(
                    first,
                    got[k][base : base + 2 * z.CS, :],
                    got[k][base + 2 * z.CS : base + 4 * z.CS, :],
                )
                for y in range(z.Y):
                    out[band * z.Y + y, :size, :] = main
                    out[band * z.Y + y, size:, :] = edge


def ring_parts(z, anc, parent, nest, buf, up, dn, tail, head, sem):
    fetch = [
        pltpu.make_async_copy(nest.at[:, :, z.H - 8 :, :], tail, sem.at[0]),
        pltpu.make_async_copy(nest.at[:, :, :8, :], head, sem.at[1]),
    ]
    for copy in fetch:
        copy.start()
    g, d = lax.axis_index("grp"), lax.axis_index("dev")
    row_base, col_base = g * z.TR, d * z.TC
    lane_t = iota((z.TR, LANES), 1)
    lane_f = iota((z.FR, LANES), 1)
    row_f = iota((z.FR, LANES), 0)
    lane_c = iota((z.C, LANES), 1)
    buf[...] = jnp.zeros_like(buf)

    def nest_ring(n, _):
        to = n // z.L
        l = n - to * z.L
        slot = to
        r, q = anc[0, n], anc[1, n]
        rows_meet = (r < row_base + z.TR) & (r + z.FR > row_base)
        cols_meet = (q < col_base + z.TC) & (q + z.FC > col_base)
        shift_r = lax.rem(row_base - r + 2 * z.G * z.TR, z.FR)
        shift_q = lax.rem(col_base - q + 2 * z.D * z.TC, z.FC)
        for side in range(2):
            col = (q - 1 if side == 0 else q + z.FC) - col_base
            first = (l * 2 + side) * z.C

            @pl.when(rows_meet & (col >= 0) & (col < z.TC))
            def _(col=col, first=first):
                acc = jnp.zeros((z.TR, LANES), F32)
                for c in range(z.C):
                    at = first + c
                    moved = pltpu.roll(parent[c], lax.rem(at - col + LANES, LANES), 1)
                    acc = jnp.where(lane_t == at, moved, acc)
                if z.FR > z.TR:
                    acc = jnp.concatenate([acc, jnp.zeros((z.FR - z.TR, LANES), F32)], axis=0)
                acc = pltpu.roll(acc, shift_r, 0)
                y = row_f + (r - row_base)
                good = (y >= 0) & (y < z.TR) & (lane_f >= first) & (lane_f < first + z.C)
                buf[slot, : z.FR, :] = jnp.where(good, acc, buf[slot, : z.FR, :])

            row = (r - 1 if side == 0 else r + z.FR) - row_base

            @pl.when(cols_meet & (row >= 0) & (row < z.TR))
            def _(row=row, first=first):
                rows = jnp.concatenate(
                    [parent[c, pl.ds(row, 1), :] for c in range(z.C)], axis=0
                )
                x = lane_c + (q - col_base)
                moved = jnp.where((x >= 0) & (x < z.TC), pltpu.roll(rows, shift_q, 1), 0.0)
                buf[slot, pl.ds(pl.multiple_of(z.FR + first, 8), z.C), :] = moved

        return 0

    lax.fori_loop(0, z.N, nest_ring, 0)
    for to in range(z.G):
        edge = jnp.where(to > g, z.TR - 1, 0)
        for c in range(z.C):
            buf[to, z.RING + c : z.RING + c + 1, :] = parent[c, pl.ds(edge, 1), :]
    first = jnp.zeros((z.TR, LANES), F32)
    last = first
    for c in range(z.C):
        first = jnp.where(lane_t == c, pltpu.roll(parent[c], c, 1) if c else parent[c], first)
        last = jnp.where(lane_t == c, pltpu.roll(parent[c], c + 1, 1), last)
    up[z.EDGE :, :] = last
    dn[z.EDGE :, :] = first
    for copy in fetch:
        copy.wait()
    for l in range(z.L):
        for c in range(z.C):
            for x in range(3):
                at = x * z.HALO + 3 * (l * z.C + c)
                lanes = slice(x * LANES, (x + 1) * LANES)
                up[at : at + 3, :] = tail[l, c, 5:8, lanes]
                dn[at : at + 3, :] = head[l, c, 0:3, lanes]


def ring_next(z, got, out, edges, slab):
    g, d = lax.axis_index("grp"), lax.axis_index("dev")
    C, L, FR, M = z.C, z.L, z.FR, z.M
    total = got[0, : z.RING, :]
    for k in range(1, z.G):
        total = total + got[k, : z.RING, :]
    slab[...] = total
    sub = iota((8, LANES), 0)
    for to in range(z.D):
        out[to, :M, :] = slab[to * M : (to + 1) * M, :]
        hi = min(to * M + M, FR - 1)
        lo = max(to * M - 1, 0)
        hi, lo = slab[hi : hi + 1, :], slab[lo : lo + 1, :]
        out[to, M:16, :] = jnp.where(sub == 0, hi, jnp.where(sub == 7, lo, 0.0))
        for l in range(L):
            at = 16 + l * C
            if to == 0 or to == z.D - 1:
                k = FR + (l * 2 + (0 if to == 0 else 1)) * C
                out[to, at : at + C, :] = slab[k : k + C, :]
            else:
                out[to, at : at + C, :] = jnp.zeros((C, LANES), F32)
    before, after = jnp.maximum(g - 1, 0), jnp.minimum(g + 1, z.G - 1)
    edges[:C, :] = jnp.where(g > 0, got[before, z.RING :, :], 0.0)
    edges[C:, :] = jnp.where(g < z.G - 1, got[after, z.RING :, :], 0.0)
    lane = iota((8, LANES), 1)
    first = jnp.zeros((8, LANES), F32)
    last = first
    for c in range(C):
        lo = edges[c : c + 1, :]
        hi = edges[C + c : C + c + 1, :]
        cap = jnp.where(sub == 0, hi, jnp.where(sub == 7, lo, 0.0))
        first = jnp.where(lane == c, pltpu.roll(cap, c, 1) if c else cap, first)
        last = jnp.where(lane == c, pltpu.roll(cap, c + 1, 1), last)
    for to in range(z.D):
        out[to, z.RG2 - 8 :, :] = jnp.where(to > d, last, first)


def nest_steps(z, diff, cour, phases, got, up_in, dn_in, out, back, ring, up, dn):
    d = lax.axis_index("dev")
    C, M = z.C, z.M
    strip = Strip()
    fine = lax.rem(iota((2 * z.W, z.W), 0), z.W)
    place = iota((2 * z.W, z.W), 1)
    deal = jnp.where(fine == lax.rem(place, LANES) * 3 + place // LANES, 1.0, 0.0).astype(BF16)
    for source, target in ((up_in, up), (dn_in, dn)):
        halo = [source[x * z.HALO : (x + 1) * z.HALO, :] for x in range(3)]
        dealt = split_dot(jnp.concatenate(halo, axis=1), deal)
        for x in range(3):
            target[x * z.HALO : (x + 1) * z.HALO, :] = dealt[:, x * LANES : (x + 1) * LANES]
    total = got[0]
    for k in range(1, z.D):
        total = total + got[k]
    ring[...] = total
    side_main = [ring[:M, :], pltpu.roll(ring[:M, :], 4, 0)]
    side_cap = jnp.where(
        strip.any_high, ring[M : M + 1, :], jnp.where(strip.any_low, ring[15:16, :], 0.0)
    )
    hold_low, hold_high = strip.any_low & (d == 0), strip.any_high & (d == z.D - 1)
    nest_1 = strip.high[1] | strip.low[1]

    def channel(c, _):
        co = weights(diff, cour, c, 3.0)
        u = [
            [[phase_rows(z, phases, l, c, y, x) for x in range(3)] for y in range(3)]
            for l in range(2)
        ]
        cap = []
        for y in range(3):
            row = []
            for x in range(3):
                v = jnp.zeros((8, LANES), F32)
                for l in range(2):
                    at = x * z.HALO + (l * C + c) * 3 + y
                    v = jnp.where(strip.high[l], dn[pl.ds(at, 1), :], v)
                    v = jnp.where(strip.low[l], up[pl.ds(at, 1), :], v)
                row.append(v)
            cap.append(row)
        u.append(cap)
        end = jnp.where(nest_1, ring[pl.ds(16 + C + c, 1), :], ring[pl.ds(16 + c, 1), :])
        west, east = [], []
        for side, lane, ghosts in ((0, 0, west), (1, LANES - 1, east)):
            turn = [lax.rem(lane - ((l * 2 + side) * C + c) + LANES, LANES) for l in range(2)]
            for l in range(2):
                ghosts.append(pltpu.roll(side_main[l], turn[l], 1))
            caps = [pltpu.roll(side_cap, turn[l], 1) for l in range(2)]
            ghosts.append(jnp.where(nest_1, caps[1], caps[0]))

        def hold(u):
            cap = [
                [jnp.where(hold_high, end, v) for v in u[2][0]],
                u[2][1],
                [jnp.where(hold_low, end, v) for v in u[2][2]],
            ]
            return [u[0], u[1], cap]

        u = hold(u)
        for k in range(3):
            u = strip.step(u, co, west, east)
            if k < 2:
                u = hold(u)
        for l in range(2):
            for y in range(3):
                for x in range(3):
                    v = u[l][y][x]
                    v = v if l == 0 else pltpu.roll(v, 4, 0)
                    back[x, pl.ds((l * C + c) * z.H + y, M, 3), :] = v
        return 0

    lax.fori_loop(0, C, channel, 0, unroll=2)
    fine = iota((2 * z.W, z.W), 1)
    place = lax.rem(iota((2 * z.W, z.W), 0), z.W)
    at = lax.rem(place, LANES) * 3 + place // LANES
    undeal = jnp.where(fine == at, 1.0, 0.0).astype(BF16)
    done = split_dot(jnp.concatenate([back[0], back[1], back[2]], axis=1), undeal)
    out[...] = done.reshape(z.L, C, z.H, z.W)


def parent_step(z, anc, diff, cour, parent, edges, up_in, dn_in, got, out):
    g, d = lax.axis_index("grp"), lax.axis_index("dev")
    C = z.C
    rows = z.TR + 8
    n = nest_at(z, anc, g // z.S * z.NB + d // z.Y)
    i = iota((z.TR, LANES), 0) + (g * z.TR - anc[0, n])
    j = iota((z.TR, LANES), 1) + (d * z.TC - anc[1, n])
    inside = (i >= 0) & (i < z.FR) & (j >= 0) & (j < z.FC)
    one = lambda cond: jnp.where(cond, 1.0, 0.0).astype(F32)
    on_w, on_e = one(inside & (j == 0)), one(inside & (j == z.FC - 1))
    on_s, on_n = one(inside & (i == 0)), one(inside & (i == z.FR - 1))
    i_end, j_end = one((i == 0) | (i == z.FR - 1)), one((j == 0) | (j == z.FC - 1))
    i_lo, i_hi = one(i > 0), one(i < z.FR - 1)
    j_lo, j_hi = one(j > 0), one(j < z.FC - 1)
    lane = iota((rows, LANES), 1)
    sub = iota((8, LANES), 0)

    cap_w = jnp.where(d > 0, got[jnp.maximum(d - 1, 0), z.RG2 - 8 :, :], 0.0)
    cap_e = jnp.where(d < z.D - 1, got[jnp.minimum(d + 1, z.D - 1), z.RG2 - 8 :, :], 0.0)
    col_w = jnp.concatenate([up_in[z.EDGE :, :], cap_w], axis=0)
    col_e = jnp.concatenate([dn_in[z.EDGE :, :], cap_e], axis=0)

    def channel(c, _):
        co = [v[:1] for v in weights(diff, cour, c, 1.0)]
        fm, fe, fw, fn, fs = [v[:1] for v in weights(diff, cour, c, 3.0)]
        lo = edges[pl.ds(c, 1), :]
        hi = edges[pl.ds(C + c, 1), :]
        cap = jnp.where(sub == 0, hi, jnp.where(sub == 7, lo, 0.0))
        full = jnp.concatenate([parent[c], cap], axis=0)
        w_in = pltpu.roll(col_w, lax.rem(LANES - c, LANES), 1)
        e_in = pltpu.roll(col_e, LANES - 1 - c, 1)
        w_all = jnp.where(lane == 0, w_in, pltpu.roll(full, 1, 1))
        e_all = jnp.where(lane == LANES - 1, e_in, pltpu.roll(full, LANES - 1, 1))
        up = lambda x: pltpu.roll(x, rows - 1, 0)[: z.TR]
        down = lambda x: pltpu.roll(x, 1, 0)[: z.TR]
        mid = full[: z.TR]
        w, e, n, s = w_all[: z.TR], e_all[: z.TR], up(full), down(full)
        w_up, w_down, e_up, e_down = up(w_all), down(w_all), up(e_all), down(e_all)
        step = (
            co[MID] * mid
            + (co[EAST] * e + co[WEST] * w)
            + (co[NORTH] * n + co[SOUTH] * s)
        )
        a, b, k, x = ghost_share(fw, fe, fm, fs, fn)
        share = on_w * ((a - x * i_end) * w + (b * i_lo) * w_down + (k * i_hi) * w_up)
        a, b, k, x = ghost_share(fe, fw, fm, fs, fn)
        share += on_e * ((a - x * i_end) * e + (b * i_lo) * e_down + (k * i_hi) * e_up)
        a, b, k, x = ghost_share(fs, fn, fm, fw, fe)
        share += on_s * ((a - x * j_end) * s + (b * j_lo) * w_down + (k * j_hi) * e_down)
        a, b, k, x = ghost_share(fn, fs, fm, fw, fe)
        share += on_n * ((a - x * j_end) * n + (b * j_lo) * w_up + (k * j_hi) * e_up)
        out[c] = jnp.where(inside, share, step)
        return 0

    lax.fori_loop(0, C, channel, 0, unroll=2)


def merge(z, which, anchor, base, pieces):
    count, size = len(which), z.CS * z.M

    def kernel(*refs):
        anc_in, base_in, refs = refs[0], refs[1], refs[2:]
        source, base_out, refs = refs[:count], refs[count], refs[count + 1 :]
        anc, refs = refs[0], refs[1:]
        inner, (old, new, twice, sem) = refs[:count], refs[count:]
        g, d = lax.axis_index("grp"), lax.axis_index("dev")
        part = lax.rem(g, z.S)
        firsts = [lax.rem(part - k + z.S, z.S) * z.CS for k in which]
        fetch = [pltpu.make_async_copy(anc_in, anc, sem.at[0])]
        for k in range(count):
            rows = base_in.at[pl.ds(firsts[k], z.CS)]
            fetch.append(pltpu.make_async_copy(source[k], inner[k], sem.at[1 + 2 * k]))
            fetch.append(pltpu.make_async_copy(rows, old.at[k], sem.at[2 + 2 * k]))
        for copy in fetch:
            copy.start()
        for copy in fetch:
            copy.wait()
        n = nest_at(z, anc, g // z.S * z.NB + d // z.Y)
        r, q = anc[0, n], anc[1, n]
        start = lax.rem(g * z.TR - r + 2 * z.G * z.TR, z.FR)
        shift_q = lax.rem(q - d * z.TC + 2 * z.D * z.TC, z.FC)
        i = iota((z.TR, LANES), 0) + (g * z.TR - r)
        j = iota((z.TR, LANES), 1) + (d * z.TC - q)
        inside = (i >= 0) & (i < z.FR) & (j >= 0) & (j < z.FC)
        sub = iota((z.M, LANES), 0)
        store = []
        for k in range(count):
            piece = inner[k]
            for c in range(z.CS):
                for m in range(z.D):
                    x = piece[m, c * z.M : (c + 1) * z.M, :]
                    if m + 1 < z.D:
                        row = piece[m + 1, size + c : size + c + 1, :]
                        x += jnp.where(sub == z.M - 1, row, 0.0)
                    if m > 0:
                        row = piece[m - 1, size + z.CS + c : size + z.CS + c + 1, :]
                        x += jnp.where(sub == 0, row, 0.0)
                    twice[c % 4, m * z.M : (m + 1) * z.M, :] = x
                    if m * z.M < z.TR:
                        twice[c % 4, z.FR + m * z.M : z.FR + (m + 1) * z.M, :] = x
                x = pltpu.roll(twice[c % 4, pl.ds(start, z.TR), :], shift_q, 1)
                new[k, c] = old[k, c] + jnp.where(inside, x, 0.0)
            rows = base_out.at[pl.ds(firsts[k], z.CS)]
            store.append(pltpu.make_async_copy(new.at[k], rows, sem.at[1 + 2 * k]))
            store[-1].start()
        for copy in store:
            copy.wait()

    place = pl.BlockSpec(memory_space=pltpu.HBM)
    half = pltpu.VMEM((count, z.CS, z.TR, LANES), F32)
    return pl.pallas_call(
        kernel,
        out_shape=jax.ShapeDtypeStruct(base.shape, F32),
        in_specs=[place] * (2 + count),
        out_specs=place,
        input_output_aliases={1: 0},
        scratch_shapes=[
            pltpu.SMEM(anchor.shape, anchor.dtype),
            *[pltpu.VMEM(x.shape, F32) for x in pieces],
            half,
            half,
            pltpu.VMEM((4, z.FR + z.TR, LANES), F32),
            pltpu.SemaphoreType.DMA((1 + 2 * count,)),
        ],
        compiler_params=pltpu.CompilerParams(vmem_limit_bytes=VMEM_LIMIT),
    )(anchor, base, *pieces)


def shards(parent, nest, anchor, diff, cour):
    z = Sizes(parent, nest, anchor, lax.axis_size("grp"), lax.axis_size("dev"))
    sds = lambda *shape: jax.ShapeDtypeStruct(shape, F32)
    vmem = lambda *shape: pltpu.VMEM(shape, F32)
    to_grp = lambda x, k: lax.ppermute(x, "grp", [(a, a ^ k) for a in range(z.G)])

    anchor = anchor.T
    message = sds(z.EDGE + z.TR, LANES)
    edge_tile = vmem(z.L, z.C, 8, z.W)
    ring, up, dn = call(
        functools.partial(ring_parts, z),
        [sds(z.G, z.RG, LANES), message, message],
        (anchor,),
        (parent,),
        [edge_tile, edge_tile, pltpu.SemaphoreType.DMA((2,))],
        (nest,),
    )
    nest, ring = lax.optimization_barrier((nest, ring))
    ring = lax.all_to_all(ring, "grp", 0, 0, tiled=True)
    *chunks, phases = call(
        functools.partial(partial_averages, z),
        [sds(z.R1, LANES)] * z.S + [sds(3, z.L * z.C * z.H, LANES)],
        (diff, cour),
        (),
        [pltpu.VMEM(nest.shape, F32), pltpu.SemaphoreType.DMA((z.L,))],
        (nest,),
        z.S,
    )
    chunks, ring, up, dn = lax.optimization_barrier((chunks, ring, up, dn))
    forward = [(k, k + 1) for k in range(z.D - 1)]
    up = lax.ppermute(up, "dev", forward)
    dn = lax.ppermute(dn, "dev", [(b, a) for a, b in forward])
    got = [chunks[0]] + [to_grp(chunks[k % z.S], k) for k in range(1, z.G)]
    ring, edges = call(
        functools.partial(ring_next, z),
        [sds(z.D, z.RG2, LANES), sds(2 * z.C, LANES)],
        (),
        (ring,),
        [vmem(z.RING, LANES)],
    )
    ring = lax.all_to_all(ring, "dev", 0, 0, tiled=True)
    (avg,) = call(functools.partial(pick_band, z), [sds(z.D, z.R2, LANES)], (anchor,), got)
    avg, phases, edges, ring, up, dn = lax.optimization_barrier(
        (avg, phases, edges, ring, up, dn)
    )
    avg = lax.all_to_all(avg, "dev", 0, 0, tiled=True)
    (out,) = call(
        functools.partial(parent_step, z),
        [jax.ShapeDtypeStruct(parent.shape, F32)],
        (anchor, diff, cour),
        (parent, edges, up, dn, ring),
    )
    (nest_out,) = call(
        functools.partial(nest_steps, z),
        [jax.ShapeDtypeStruct(nest.shape, F32)],
        (diff, cour),
        (phases, ring, up, dn),
        [
            vmem(3, z.L * z.C * z.H, LANES),
            vmem(z.RG2, LANES),
            vmem(z.EDGE, LANES),
            vmem(z.EDGE, LANES),
        ],
    )
    avg, nest_out, out = lax.optimization_barrier((avg, nest_out, out))
    pieces = [avg]
    for k in range(1, z.S):
        pairs = [(a, a // z.S * z.S + (a + k) % z.S) for a in range(z.G)]
        pieces.append(lax.ppermute(avg, "grp", pairs))
    for which in ([0], list(range(1, z.S))):
        out = merge(z, which, anchor, out, [pieces[k] for k in which])
    return out, nest_out


def solution(mesh):
    placed = (P(None, "grp", "dev"), P("grp", None, "dev", None), P(), P(), P())
    return jax.shard_map(
        shards,
        mesh=mesh,
        in_specs=placed,
        out_specs=(P(None, "grp", "dev"), P("grp", None, "dev", None)),
        check_vma=False,
    )
```

profile of v0, /device:TPU:0, one launch (start us, length us, event | category | flops | bytes accessed | tf_op | source)
XLA Modules:
  0.0 67.8 jit_solution(7223412704121648786)
XLA Ops:
  0.6 3.4 %shard_map.68 = (f32[4,184,128]{2,1,0:T(8,128)}, f32[496,128]{1,0:T(8,128)}, f32[496,128]{1,0:T(8,128)}) custom-call(s32[2,8]{1,0:T(2,128)} %bitcast.1, f32[24,64,128]{2,1,0:T(8,128)} %refs_3_.1, f32[2,24,24,384]{3,2,1,0:T(8,128)} %refs_2_.3), custom_call_target="tpu_custom_call" | custom-call | tf_op jit(solution)/shard_map/pallas_call | solution.py:71
  4.0 4.2 %all-to-all-start = ((f32[4,184,128]{2,1,0:T(8,128)}), f32[4,184,128]{2,1,0:T(8,128)S(1)}, u32[]{:S(2)}, u32[]{:S(2)}) async-start(f32[4,184,128]{2,1,0:T(8,128)} %get-tuple-element.30), calls=%async_computation | async-start | bytes 753664 | tf_op jit(solution)/shard_map/all_to_all | solution.py:626
  8.2 7.3 %shard_map.69 = (f32[240,128]{1,0:T(8,128)}, f32[240,128]{1,0:T(8,128)}, f32[3,1152,128]{2,1,0:T(8,128)}) custom-call(f32[2,24]{1,0:T(2,128)} %refs_1_.7, f32[2,24]{1,0:T(2,128)} %refs_2_.4, f32[2,24,24,384]{3,2,1,0:T(8,128)} %refs_2_.3), custom_call_target="tpu_custom_call" | custom-call | tf_op jit(solution)/shard_map/pallas_call | solution.py:71
  15.5 0.0 all-to-all-done.refs_0_
  15.5 0.0 copy-start.2
  15.6 0.7 %copy-done.2 = f32[4,184,128]{2,1,0:T(8,128)} copy-done((f32[4,184,128]{2,1,0:T(8,128)}, f32[4,184,128]{2,1,0:T(8,128)S(1)}, u32[]{:S(2)}) %copy-start.2) | copy-done | bytes 376856
  16.3 1.9 %shard_map.71 = (f32[8,72,128]{2,1,0:T(8,128)}, f32[48,128]{1,0:T(8,128)}) custom-call(f32[4,184,128]{2,1,0:T(8,128)} %copy-done.2), custom_call_target="tpu_custom_call" | custom-call | tf_op jit(solution)/shard_map/pallas_call | solution.py:71
  18.2 6.6 %all-to-all-start.1 = ((f32[8,72,128]{2,1,0:T(8,128)}), f32[8,72,128]{2,1,0:T(8,128)S(1)}, u32[]{:S(2)}, u32[]{:S(2)}) async-start(f32[8,72,128]{2,1,0:T(8,128)} %get-tuple-element.38), calls=%async_computation.1 | async-start | bytes 589824 | tf_op jit(solution)/shard_map/all_to_all | solution.py:648
  24.7 3.9 %collective-permute-start.3 = (f32[496,128]{1,0:T(8,128)}, f32[496,128]{1,0:T(8,128)S(1)}, u32[]{:S(2)}, u32[]{:S(2)}) collective-permute-start(f32[496,128]{1,0:T(8,128)} %get-tuple-element.39), channel_id=1, source_target_pairs={{0,1},{1,2},{2,3},{3,4},{4,5},{5,6},{6,7},{8,9},{9,10},{10,11},{11... | collective-permute-start | bytes 761864 | tf_op jit(solution)/shard_map/ppermute | solution.py:638
  28.7 1.3 %collective-permute-start.4 = (f32[496,128]{1,0:T(8,128)}, f32[496,128]{1,0:T(8,128)S(1)}, u32[]{:S(2)}, u32[]{:S(2)}) collective-permute-start(f32[496,128]{1,0:T(8,128)} %get-tuple-element.40), channel_id=1, source_target_pairs={{1,0},{2,1},{3,2},{4,3},{5,4},{6,5},{7,6},{9,8},{10,9},{11,10},{12... | collective-permute-start | bytes 761864 | tf_op jit(solution)/shard_map/ppermute | solution.py:639
  30.0 0.1 collective-permute-start
  30.0 2.0 %collective-permute-start.1 = (f32[240,128]{1,0:T(8,128)}, f32[240,128]{1,0:T(8,128)}, u32[]{:S(2)}, u32[]{:S(2)}) collective-permute-start(f32[240,128]{1,0:T(8,128)} %get-tuple-element.33.refs_1_), channel_id=1, source_target_pairs={{0,16},{8,24},{16,0},{24,8},{1,17},{9,25},{17,1},{25,9},{2,18},{10... | collective-permute-start | bytes 368648 | tf_op jit(solution)/shard_map/ppermute | solution.py:612
  32.1 0.1 collective-permute-start.2
  32.2 0.0 collective-permute-done.refs_2_
  32.2 0.0 copy-start.5
  32.2 4.5 %collective-permute-done.1.refs_3_ = f32[240,128]{1,0:T(8,128)} collective-permute-done((f32[240,128]{1,0:T(8,128)}, f32[240,128]{1,0:T(8,128)}, u32[]{:S(2)}, u32[]{:S(2)}) %collective-permute-start.1) | collective-permute-done | bytes 122912 | tf_op jit(solution)/shard_map/ppermute | solution.py:612
  36.6 2.0 %collective-permute-done.2.refs_4_ = f32[240,128]{1,0:T(8,128)} collective-permute-done((f32[240,128]{1,0:T(8,128)}, f32[240,128]{1,0:T(8,128)}, u32[]{:S(2)}, u32[]{:S(2)}) %collective-permute-start.2) | collective-permute-done | bytes 122912 | tf_op jit(solution)/shard_map/ppermute | solution.py:612
  38.6 0.0 copy-done.5
  38.7 2.3 %shard_map.70 = f32[8,120,128]{2,1,0:T(8,128)} custom-call(s32[2,8]{1,0:T(2,128)} %bitcast.2, f32[240,128]{1,0:T(8,128)} %get-tuple-element.33.refs_1_, f32[240,128]{1,0:T(8,128)} %copy-done.5, f32[240,128]{1,0:T(8,128)} %collective-permute-done.1.refs_3_, f32[240,128]{1,0:T(8,128)} %collective-permute-done.2.refs_4_), custom_call_target="tpu_custom_call" | custom-call | tf_op jit(solution)/shard_map/pallas_call | solution.py:71
  40.9 0.3 collective-permute-done.3.refs_4_.refs_5_
  41.2 0.0 copy-start.3
  41.2 0.0 collective-permute-done.4.refs_5_.refs_6_
  41.2 0.0 copy-start.4
  41.2 0.0 all-to-all-done.1.refs_3_.refs_7_
  41.2 0.0 copy-start
  41.2 0.7 %copy-done.3 = f32[496,128]{1,0:T(8,128)} copy-done((f32[496,128]{1,0:T(8,128)}, f32[496,128]{1,0:T(8,128)S(1)}, u32[]{:S(2)}) %copy-start.3) | copy-done | bytes 253976
  41.9 0.1 copy-done.4
  42.0 6.3 %all-to-all-start.2 = ((f32[8,120,128]{2,1,0:T(8,128)}), f32[8,120,128]{2,1,0:T(8,128)S(1)}, u32[]{:S(2)}, u32[]{:S(2)}) async-start(f32[8,120,128]{2,1,0:T(8,128)} %shard_map.70), calls=%async_computation.2 | async-start | bytes 983040 | tf_op jit(solution)/shard_map/all_to_all | solution.py:653
  48.4 0.0 copy-done
  48.4 8.3 %shard_map.72 = f32[2,24,24,384]{3,2,1,0:T(8,128)} custom-call(f32[2,24]{1,0:T(2,128)} %refs_1_.7, f32[2,24]{1,0:T(2,128)} %refs_2_.4, f32[3,1152,128]{2,1,0:T(8,128)} %get-tuple-element.42.refs_2_, f32[8,72,128]{2,1,0:T(8,128)} %copy-done, f32[496,128]{1,0:T(8,128)} %copy-done.3, f32[496,128]{1,0:T(8,128)} %copy-done.4), custom_call_target="tpu_custom_call" | custom-call | tf_op jit(solution)/shard_map/pallas_call | solution.py:71
  56.7 5.1 %shard_map.73.refs_1_ = f32[24,64,128]{2,1,0:T(8,128)} custom-call(s32[2,8]{1,0:T(2,128)} %bitcast.3, f32[2,24]{1,0:T(2,128)} %refs_1_.7, f32[2,24]{1,0:T(2,128)} %refs_2_.4, f32[24,64,128]{2,1,0:T(8,128)} %refs_3_.1, f32[48,128]{1,0:T(8,128)} %get-tuple-element.46.refs_4_, f32[496,128]{1,0:T(8,128)} %copy-done.3, f32[496,128]{1,0:T(8,128)} %copy-done.4, ...), custom_call_target="tpu_custom_call" | custom-call | tf_op jit(solution)/shard_map/pallas_call | solution.py:71
  61.8 0.8 %all-to-all-done.2.refs_2_ = f32[8,120,128]{2,1,0:T(8,128)S(1)} async-done(((f32[8,120,128]{2,1,0:T(8,128)}), f32[8,120,128]{2,1,0:T(8,128)S(1)}, u32[]{:S(2)}, u32[]{:S(2)}) %all-to-all-start.2) | async-done | bytes 491552 | tf_op jit(solution)/shard_map/all_to_all | solution.py:653
  62.6 0.0 copy-start.1
  62.6 0.0 collective-permute-start.5
  62.6 0.8 %copy-done.1 = f32[8,120,128]{2,1,0:T(8,128)} copy-done((f32[8,120,128]{2,1,0:T(8,128)}, f32[8,120,128]{2,1,0:T(8,128)S(1)}, u32[]{:S(2)}) %copy-start.1) | copy-done | bytes 491544
  63.4 2.2 %shard_map.74.refs_1_ = f32[24,64,128]{2,1,0:T(8,128)} custom-call(s32[2,8]{1,0:T(2,128)} %bitcast.4, f32[24,64,128]{2,1,0:T(8,128)} %shard_map.73.refs_1_, f32[8,120,128]{2,1,0:T(8,128)} %copy-done.1), custom_call_target="tpu_custom_call", output_to_operand_aliasing={{}: (1, {})} | custom-call | tf_op jit(solution)/shard_map/pallas_call | solution.py:590
  65.6 0.0 collective-permute-done.5.refs_2_
  65.6 2.2 %shard_map.75 = f32[24,64,128]{2,1,0:T(8,128)} custom-call(s32[2,8]{1,0:T(2,128)} %bitcast.5, f32[24,64,128]{2,1,0:T(8,128)} %shard_map.74.refs_1_, f32[8,120,128]{2,1,0:T(8,128)} %collective-permute-done.5.refs_2_), custom_call_target="tpu_custom_call", output_to_operand_aliasing={{}: (1, {})} | custom-call | tf_op jit(solution)/shard_map/pallas_call | solution.py:590
Async XLA Ops:
  4.0 11.5 %all-to-all-start = ((f32[4,184,128]{2,1,0:T(8,128)}), f32[4,184,128]{2,1,0:T(8,128)S(1)}, u32[]{:S(2)}, u32[]{:S(2)}) async-start(f32[4,184,128]{2,1,0:T(8,128)} %get-tuple-element.30), calls=%async_computation | async-start | bytes 753664 | tf_op jit(solution)/shard_map/all_to_all | solution.py:626
  15.5 0.7 %copy-start.2 = (f32[4,184,128]{2,1,0:T(8,128)}, f32[4,184,128]{2,1,0:T(8,128)S(1)}, u32[]{:S(2)}) copy-start(f32[4,184,128]{2,1,0:T(8,128)S(1)} %all-to-all-done.refs_0_) | copy-start | bytes 1130500
  18.2 23.1 %all-to-all-start.1 = ((f32[8,72,128]{2,1,0:T(8,128)}), f32[8,72,128]{2,1,0:T(8,128)S(1)}, u32[]{:S(2)}, u32[]{:S(2)}) async-start(f32[8,72,128]{2,1,0:T(8,128)} %get-tuple-element.38), calls=%async_computation.1 | async-start | bytes 589824 | tf_op jit(solution)/shard_map/all_to_all | solution.py:648
  24.7 16.5 %collective-permute-start.3 = (f32[496,128]{1,0:T(8,128)}, f32[496,128]{1,0:T(8,128)S(1)}, u32[]{:S(2)}, u32[]{:S(2)}) collective-permute-start(f32[496,128]{1,0:T(8,128)} %get-tuple-element.39), channel_id=1, source_target_pairs={{0,1},{1,2},{2,3},{3,4},{4,5},{5,6},{6,7},{8,9},{9,10},{10,11},{11... | collective-permute-start | bytes 761864 | tf_op jit(solution)/shard_map/ppermute | solution.py:638
  28.7 12.5 %collective-permute-start.4 = (f32[496,128]{1,0:T(8,128)}, f32[496,128]{1,0:T(8,128)S(1)}, u32[]{:S(2)}, u32[]{:S(2)}) collective-permute-start(f32[496,128]{1,0:T(8,128)} %get-tuple-element.40), channel_id=1, source_target_pairs={{1,0},{2,1},{3,2},{4,3},{5,4},{6,5},{7,6},{9,8},{10,9},{11,10},{12... | collective-permute-start | bytes 761864 | tf_op jit(solution)/shard_map/ppermute | solution.py:639
  30.0 2.2 %collective-permute-start = (f32[240,128]{1,0:T(8,128)}, f32[240,128]{1,0:T(8,128)S(1)}, u32[]{:S(2)}, u32[]{:S(2)}) collective-permute-start(f32[240,128]{1,0:T(8,128)} %get-tuple-element.34), channel_id=1, source_target_pairs={{0,8},{8,0},{16,24},{24,16},{1,9},{9,1},{17,25},{25,17},{2,10},{10... | collective-permute-start | bytes 368648 | tf_op jit(solution)/shard_map/ppermute | solution.py:612
  30.0 6.6 %collective-permute-start.1 = (f32[240,128]{1,0:T(8,128)}, f32[240,128]{1,0:T(8,128)}, u32[]{:S(2)}, u32[]{:S(2)}) collective-permute-start(f32[240,128]{1,0:T(8,128)} %get-tuple-element.33.refs_1_), channel_id=1, source_target_pairs={{0,16},{8,24},{16,0},{24,8},{1,17},{9,25},{17,1},{25,9},{2,18},{10... | collective-permute-start | bytes 368648 | tf_op jit(solution)/shard_map/ppermute | solution.py:612
  32.1 6.6 %collective-permute-start.2 = (f32[240,128]{1,0:T(8,128)}, f32[240,128]{1,0:T(8,128)}, u32[]{:S(2)}, u32[]{:S(2)}) collective-permute-start(f32[240,128]{1,0:T(8,128)} %get-tuple-element.34), channel_id=1, source_target_pairs={{0,24},{8,16},{16,8},{24,0},{1,25},{9,17},{17,9},{25,1},{2,26},{10... | collective-permute-start | bytes 368648 | tf_op jit(solution)/shard_map/ppermute | solution.py:612
  32.2 6.5 %copy-start.5 = (f32[240,128]{1,0:T(8,128)}, f32[240,128]{1,0:T(8,128)S(1)}, u32[]{:S(2)}) copy-start(f32[240,128]{1,0:T(8,128)S(1)} %collective-permute-done.refs_2_) | copy-start | bytes 368644
  41.2 0.7 %copy-start.3 = (f32[496,128]{1,0:T(8,128)}, f32[496,128]{1,0:T(8,128)S(1)}, u32[]{:S(2)}) copy-start(f32[496,128]{1,0:T(8,128)S(1)} %collective-permute-done.3.refs_4_.refs_5_) | copy-start | bytes 761860
  41.2 0.8 %copy-start.4 = (f32[496,128]{1,0:T(8,128)}, f32[496,128]{1,0:T(8,128)S(1)}, u32[]{:S(2)}) copy-start(f32[496,128]{1,0:T(8,128)S(1)} %collective-permute-done.4.refs_5_.refs_6_) | copy-start | bytes 761860
  41.2 7.1 %copy-start = (f32[8,72,128]{2,1,0:T(8,128)}, f32[8,72,128]{2,1,0:T(8,128)S(1)}, u32[]{:S(2)}) copy-start(f32[8,72,128]{2,1,0:T(8,128)S(1)} %all-to-all-done.1.refs_3_.refs_7_) | copy-start | bytes 884740
  42.0 20.6 %all-to-all-start.2 = ((f32[8,120,128]{2,1,0:T(8,128)}), f32[8,120,128]{2,1,0:T(8,128)S(1)}, u32[]{:S(2)}, u32[]{:S(2)}) async-start(f32[8,120,128]{2,1,0:T(8,128)} %shard_map.70), calls=%async_computation.2 | async-start | bytes 983040 | tf_op jit(solution)/shard_map/all_to_all | solution.py:653
  62.6 0.8 %copy-start.1 = (f32[8,120,128]{2,1,0:T(8,128)}, f32[8,120,128]{2,1,0:T(8,128)S(1)}, u32[]{:S(2)}) copy-start(f32[8,120,128]{2,1,0:T(8,128)S(1)} %all-to-all-done.2.refs_2_) | copy-start | bytes 1474564
  62.6 3.0 %collective-permute-start.5 = (f32[8,120,128]{2,1,0:T(8,128)S(1)}, f32[8,120,128]{2,1,0:T(8,128)}, u32[]{:S(2)}, u32[]{:S(2)}) collective-permute-start(f32[8,120,128]{2,1,0:T(8,128)S(1)} %all-to-all-done.2.refs_2_), channel_id=1, source_target_pairs={{0,8},{8,0},{16,24},{24,16},{1,9},{9,1},{17,25},{25,17},{2,10},{10... | collective-permute-start | bytes 1474568 | tf_op jit(solution)/shard_map/ppermute | solution.py:676
where the time goes:
time: 68.5 us; the launch traced here: 67.8 us
  Pallas kernels  32.6 us (48%)
  starting transfers between devices  24.5 us (36%)
  waiting for transfers between devices  7.6 us (11%)
  local copies, waits for them, and re-layouts  2.32 us (3%)
  between operations  0.76 us (1%)
    pallas_call x6, Pallas kernels, call(): pl.pallas_call(kernel, out_shape=list(out_shape), in_specs=[place] * (n_i...  28.2 us
    all_to_all x1, starting transfers between devices, shards(): ring = lax.all_to_all(ring, 'dev', 0, 0, tiled=True)  6.57 us
    ppermute x3, waiting for transfers between devices, shards(): lax.ppermute(x, 'grp', [(a, a ^ k) for a in range(z.G)])  6.49 us
    all_to_all x1, starting transfers between devices, shards(): avg = lax.all_to_all(avg, 'dev', 0, 0, tiled=True)  6.35 us
    pallas_call x2, Pallas kernels, merge(): pl.pallas_call(kernel, out_shape=jax.ShapeDtypeStruct(base.shape, F32), i...  4.42 us
    all_to_all x1, starting transfers between devices, shards(): ring = lax.all_to_all(ring, 'grp', 0, 0, tiled=True)  4.22 us
    ppermute x1, starting transfers between devices, shards(): up = lax.ppermute(up, 'dev', forward)  3.93 us
    unnamed x12, local copies, waits for them, and re-layouts  2.32 us
  transfers between devices with their start and end apart: 9, of which 4 were waited for; matrix products, arithmetic and copies ran while one was open for 0% of the time, Pallas kernels for 37%

commit v1 on v0

--- a/solution.py
+++ b/solution.py
@@ -10,7 +10,7 @@
 F32 = jnp.float32
 BF16 = jnp.bfloat16
 LANES = 128
-VMEM_LIMIT = 63 * 1024 * 1024
+VMEM_LIMIT = 65408 * 1024
 MID, EAST, WEST, NORTH, SOUTH = range(5)
 
 
@@ -532,6 +532,15 @@
         return 0
 
     lax.fori_loop(0, C, channel, 0, unroll=2)
+
+
+def both_steps(
+    z, anc, diff, cour, parent, edges, up, dn, ring, phases, out, nest_out, *scratch_and_store
+):
+    *scratch, store_parent = scratch_and_store
+    parent_step(z, anc, diff, cour, parent, edges, up, dn, ring, out)
+    store_parent()
+    nest_steps(z, diff, cour, phases, ring, up, dn, nest_out, *scratch)
 
 
 def merge(z, which, anchor, base, pieces):
@@ -651,23 +660,19 @@
         (avg, phases, edges, ring, up, dn)
     )
     avg = lax.all_to_all(avg, "dev", 0, 0, tiled=True)
-    (out,) = call(
-        functools.partial(parent_step, z),
-        [jax.ShapeDtypeStruct(parent.shape, F32)],
+    out, nest_out = call(
+        functools.partial(both_steps, z),
+        [jax.ShapeDtypeStruct(parent.shape, F32), jax.ShapeDtypeStruct(nest.shape, F32)],
         (anchor, diff, cour),
-        (parent, edges, up, dn, ring),
-    )
-    (nest_out,) = call(
-        functools.partial(nest_steps, z),
-        [jax.ShapeDtypeStruct(nest.shape, F32)],
-        (diff, cour),
-        (phases, ring, up, dn),
+        (parent, edges, up, dn, ring, phases),
         [
             vmem(3, z.L * z.C * z.H, LANES),
             vmem(z.RG2, LANES),
             vmem(z.EDGE, LANES),
             vmem(z.EDGE, LANES),
         ],
+        (),
+        0,
     )
     avg, nest_out, out = lax.optimization_barrier((avg, nest_out, out))
     pieces = [avg]

time: 68.5 us -> 66.5 us (0.971)
  local copies, waits for them, and re-layouts: 2.32 us -> 0 us
  Pallas kernels: 32.6 us -> 30.5 us
  waiting for transfers between devices: 7.6 us -> 9.02 us
  starting transfers between devices: 24.5 us -> 25.6 us
    unnamed x12 -> x0, local copies, waits for them, and re-layouts: 2.32 us -> none
    pallas_call x6 -> x5, Pallas kernels: 28.2 us -> 26.1 us  [call(): pl.pallas_call(kernel, out_shape=list(out_shape), in_specs=[place] * (n_i...]
    all_to_all x1, waiting for transfers between devices: 0.82 us -> 2.43 us  [shards(): avg = lax.all_to_all(avg, 'dev', 0, 0, tiled=True)]
    ppermute x3, waiting for transfers between devices: 6.49 us -> 5.67 us  [shards(): lax.ppermute(x, 'grp', [(a, a ^ k) for a in range(z.G)])]
    ppermute x1, starting transfers between devices: 3.93 us -> 4.62 us  [shards(): up = lax.ppermute(up, 'dev', forward)]
  transfers between devices with their start and end apart: 9 -> 9, of which waited for: 4 -> 5; matrix products, arithmetic and copies ran while one was open for 0% -> 0% of each run, Pallas kernels for 37% -> 35%
where the time goes in v1:
time: 66.5 us; the launch traced here: 65.8 us
  Pallas kernels  30.5 us (46%)
  starting transfers between devices  25.6 us (38%)
  waiting for transfers between devices  9.02 us (14%)
  between operations  0.7 us (1%)
    pallas_call x5, Pallas kernels, call(): pl.pallas_call(kernel, out_shape=list(out_shape), in_specs=[place] * (n_i...  26.1 us
    all_to_all x1, starting transfers between devices, shards(): ring = lax.all_to_all(ring, 'dev', 0, 0, tiled=True)  6.7 us
    all_to_all x1, starting transfers between devices, shards(): avg = lax.all_to_all(avg, 'dev', 0, 0, tiled=True)  6.55 us
    ppermute x3, waiting for transfers between devices, shards(): lax.ppermute(x, 'grp', [(a, a ^ k) for a in range(z.G)])  5.67 us
    ppermute x1, starting transfers between devices, shards(): up = lax.ppermute(up, 'dev', forward)  4.62 us
    pallas_call x2, Pallas kernels, merge(): pl.pallas_call(kernel, out_shape=jax.ShapeDtypeStruct(base.shape, F32), i...  4.42 us
    all_to_all x1, starting transfers between devices, shards(): ring = lax.all_to_all(ring, 'grp', 0, 0, tiled=True)  4.22 us
    all_to_all x1, waiting for transfers between devices, shards(): avg = lax.all_to_all(avg, 'dev', 0, 0, tiled=True)  2.43 us
  transfers between devices with their start and end apart: 9, of which 5 were waited for; matrix products, arithmetic and copies ran while one was open for 0% of the time, Pallas kernels for 35%

profile of v1, /device:TPU:0, one launch (start us, length us, event | category | flops | bytes accessed | tf_op | source)
XLA Modules:
  0.0 65.8 jit_solution(8156381091122375046)
XLA Ops:
  0.6 3.4 %shard_map.68 = (f32[4,184,128]{2,1,0:T(8,128)}, f32[496,128]{1,0:T(8,128)}, f32[496,128]{1,0:T(8,128)}) custom-call(s32[2,8]{1,0:T(2,128)} %bitcast.1, f32[24,64,128]{2,1,0:T(8,128)} %refs_3_.1, f32[2,24,24,384]{3,2,1,0:T(8,128)} %refs_2_.3), custom_call_target="tpu_custom_call" | custom-call | tf_op jit(solution)/shard_map/pallas_call | solution.py:71
  4.0 4.2 %all-to-all-start = ((f32[4,184,128]{2,1,0:T(8,128)}), f32[4,184,128]{2,1,0:T(8,128)}, u32[]{:S(2)}, u32[]{:S(2)}) async-start(f32[4,184,128]{2,1,0:T(8,128)} %get-tuple-element.32), calls=%async_computation | async-start | bytes 753664 | tf_op jit(solution)/shard_map/all_to_all | solution.py:635
  8.2 7.3 %shard_map.69 = (f32[240,128]{1,0:T(8,128)}, f32[240,128]{1,0:T(8,128)}, f32[3,1152,128]{2,1,0:T(8,128)}) custom-call(f32[2,24]{1,0:T(2,128)} %refs_1_.5, f32[2,24]{1,0:T(2,128)} %refs_2_.4, f32[2,24,24,384]{3,2,1,0:T(8,128)} %refs_2_.3), custom_call_target="tpu_custom_call" | custom-call | tf_op jit(solution)/shard_map/pallas_call | solution.py:71
  15.5 0.5 all-to-all-done.refs_0_
  16.0 1.9 %shard_map.71 = (f32[8,72,128]{2,1,0:T(8,128)}, f32[48,128]{1,0:T(8,128)}) custom-call(f32[4,184,128]{2,1,0:T(8,128)} %all-to-all-done.refs_0_), custom_call_target="tpu_custom_call" | custom-call | tf_op jit(solution)/shard_map/pallas_call | solution.py:71
  17.9 6.7 %all-to-all-start.1 = ((f32[8,72,128]{2,1,0:T(8,128)}), f32[8,72,128]{2,1,0:T(8,128)}, u32[]{:S(2)}, u32[]{:S(2)}) async-start(f32[8,72,128]{2,1,0:T(8,128)} %get-tuple-element.40), calls=%async_computation.1 | async-start | bytes 589824 | tf_op jit(solution)/shard_map/all_to_all | solution.py:657
  24.6 4.6 %collective-permute-start.3 = (f32[496,128]{1,0:T(8,128)}, f32[496,128]{1,0:T(8,128)}, u32[]{:S(2)}, u32[]{:S(2)}) collective-permute-start(f32[496,128]{1,0:T(8,128)} %get-tuple-element.41), channel_id=1, source_target_pairs={{0,1},{1,2},{2,3},{3,4},{4,5},{5,6},{6,7},{8,9},{9,10},{10,11},{11... | collective-permute-start | bytes 761864 | tf_op jit(solution)/shard_map/ppermute | solution.py:647
  29.2 1.3 %collective-permute-start.4 = (f32[496,128]{1,0:T(8,128)}, f32[496,128]{1,0:T(8,128)}, u32[]{:S(2)}, u32[]{:S(2)}) collective-permute-start(f32[496,128]{1,0:T(8,128)} %get-tuple-element.42), channel_id=1, source_target_pairs={{1,0},{2,1},{3,2},{4,3},{5,4},{6,5},{7,6},{9,8},{10,9},{11,10},{12... | collective-permute-start | bytes 761864 | tf_op jit(solution)/shard_map/ppermute | solution.py:648
  30.5 2.0 %collective-permute-start.1 = (f32[240,128]{1,0:T(8,128)}, f32[240,128]{1,0:T(8,128)}, u32[]{:S(2)}, u32[]{:S(2)}) collective-permute-start(f32[240,128]{1,0:T(8,128)} %get-tuple-element.35.refs_1_), channel_id=1, source_target_pairs={{0,16},{8,24},{16,0},{24,8},{1,17},{9,25},{17,1},{25,9},{2,18},{10... | collective-permute-start | bytes 368648 | tf_op jit(solution)/shard_map/ppermute | solution.py:621
  32.6 0.0 collective-permute-start.2
  32.6 0.2 collective-permute-start
  32.8 3.5 %collective-permute-done.1.refs_3_ = f32[240,128]{1,0:T(8,128)} collective-permute-done((f32[240,128]{1,0:T(8,128)}, f32[240,128]{1,0:T(8,128)}, u32[]{:S(2)}, u32[]{:S(2)}) %collective-permute-start.1) | collective-permute-done | bytes 122912 | tf_op jit(solution)/shard_map/ppermute | solution.py:621
  36.2 2.2 %collective-permute-done.2.refs_4_ = f32[240,128]{1,0:T(8,128)} collective-permute-done((f32[240,128]{1,0:T(8,128)}, f32[240,128]{1,0:T(8,128)}, u32[]{:S(2)}, u32[]{:S(2)}) %collective-permute-start.2) | collective-permute-done | bytes 122912 | tf_op jit(solution)/shard_map/ppermute | solution.py:621
  38.4 0.0 collective-permute-done.refs_2_
  38.4 2.3 %shard_map.70 = f32[8,120,128]{2,1,0:T(8,128)} custom-call(s32[2,8]{1,0:T(2,128)} %bitcast.2, f32[240,128]{1,0:T(8,128)} %get-tuple-element.35.refs_1_, f32[240,128]{1,0:T(8,128)} %collective-permute-done.refs_2_, f32[240,128]{1,0:T(8,128)} %collective-permute-done.1.refs_3_, f32[240,128]{1,0:T(8,128)} %collective-permute-done.2.refs_4_), custom_call_target="tpu_custom_call" | custom-call | tf_op jit(solution)/shard_map/pallas_call | solution.py:71
  40.7 0.4 collective-permute-done.3.refs_5_
  41.1 0.0 collective-permute-done.4.refs_6_
  41.1 0.0 all-to-all-done.1.refs_7_
  41.1 6.5 %all-to-all-start.2 = ((f32[8,120,128]{2,1,0:T(8,128)}), f32[8,120,128]{2,1,0:T(8,128)}, u32[]{:S(2)}, u32[]{:S(2)}) async-start(f32[8,120,128]{2,1,0:T(8,128)} %shard_map.70), calls=%async_computation.2 | async-start | bytes 983040 | tf_op jit(solution)/shard_map/all_to_all | solution.py:662
  47.6 11.3 %shard_map.72 = (f32[24,64,128]{2,1,0:T(8,128)}, f32[2,24,24,384]{3,2,1,0:T(8,128)}) custom-call(s32[2,8]{1,0:T(2,128)} %bitcast.3, f32[2,24]{1,0:T(2,128)} %refs_1_.5, f32[2,24]{1,0:T(2,128)} %refs_2_.4, f32[24,64,128]{2,1,0:T(8,128)} %refs_3_.1, f32[48,128]{1,0:T(8,128)} %get-tuple-element.44.refs_4_, f32[496,128]{1,0:T(8,128)} %collective-permute-done.3.refs_5_, ...), custom_call_target="tpu_custom_call" | custom-call | tf_op jit(solution)/shard_map/pallas_call | solution.py:71
  59.0 2.4 %all-to-all-done.2.refs_2_ = f32[8,120,128]{2,1,0:T(8,128)} async-done(((f32[8,120,128]{2,1,0:T(8,128)}), f32[8,120,128]{2,1,0:T(8,128)}, u32[]{:S(2)}, u32[]{:S(2)}) %all-to-all-start.2) | async-done | bytes 491552 | tf_op jit(solution)/shard_map/all_to_all | solution.py:662
  61.4 0.0 collective-permute-start.5
  61.4 2.2 %shard_map.73.refs_1_ = f32[24,64,128]{2,1,0:T(8,128)} custom-call(s32[2,8]{1,0:T(2,128)} %bitcast.4, f32[24,64,128]{2,1,0:T(8,128)} %get-tuple-element.51.refs_1_, f32[8,120,128]{2,1,0:T(8,128)} %all-to-all-done.2.refs_2_), custom_call_target="tpu_custom_call", output_to_operand_aliasing={{}: (1, {})} | custom-call | tf_op jit(solution)/shard_map/pallas_call | solution.py:599
  63.6 0.0 collective-permute-done.5.refs_2_
  63.6 2.2 %shard_map.74 = f32[24,64,128]{2,1,0:T(8,128)} custom-call(s32[2,8]{1,0:T(2,128)} %bitcast.5, f32[24,64,128]{2,1,0:T(8,128)} %shard_map.73.refs_1_, f32[8,120,128]{2,1,0:T(8,128)} %collective-permute-done.5.refs_2_), custom_call_target="tpu_custom_call", output_to_operand_aliasing={{}: (1, {})} | custom-call | tf_op jit(solution)/shard_map/pallas_call | solution.py:599
Async XLA Ops:
  4.0 12.1 %all-to-all-start = ((f32[4,184,128]{2,1,0:T(8,128)}), f32[4,184,128]{2,1,0:T(8,128)}, u32[]{:S(2)}, u32[]{:S(2)}) async-start(f32[4,184,128]{2,1,0:T(8,128)} %get-tuple-element.32), calls=%async_computation | async-start | bytes 753664 | tf_op jit(solution)/shard_map/all_to_all | solution.py:635
  17.9 23.1 %all-to-all-start.1 = ((f32[8,72,128]{2,1,0:T(8,128)}), f32[8,72,128]{2,1,0:T(8,128)}, u32[]{:S(2)}, u32[]{:S(2)}) async-start(f32[8,72,128]{2,1,0:T(8,128)} %get-tuple-element.40), calls=%async_computation.1 | async-start | bytes 589824 | tf_op jit(solution)/shard_map/all_to_all | solution.py:657
  24.6 16.4 %collective-permute-start.3 = (f32[496,128]{1,0:T(8,128)}, f32[496,128]{1,0:T(8,128)}, u32[]{:S(2)}, u32[]{:S(2)}) collective-permute-start(f32[496,128]{1,0:T(8,128)} %get-tuple-element.41), channel_id=1, source_target_pairs={{0,1},{1,2},{2,3},{3,4},{4,5},{5,6},{6,7},{8,9},{9,10},{10,11},{11... | collective-permute-start | bytes 761864 | tf_op jit(solution)/shard_map/ppermute | solution.py:647
  29.2 11.8 %collective-permute-start.4 = (f32[496,128]{1,0:T(8,128)}, f32[496,128]{1,0:T(8,128)}, u32[]{:S(2)}, u32[]{:S(2)}) collective-permute-start(f32[496,128]{1,0:T(8,128)} %get-tuple-element.42), channel_id=1, source_target_pairs={{1,0},{2,1},{3,2},{4,3},{5,4},{6,5},{7,6},{9,8},{10,9},{11,10},{12... | collective-permute-start | bytes 761864 | tf_op jit(solution)/shard_map/ppermute | solution.py:648
  30.5 5.7 %collective-permute-start.1 = (f32[240,128]{1,0:T(8,128)}, f32[240,128]{1,0:T(8,128)}, u32[]{:S(2)}, u32[]{:S(2)}) collective-permute-start(f32[240,128]{1,0:T(8,128)} %get-tuple-element.35.refs_1_), channel_id=1, source_target_pairs={{0,16},{8,24},{16,0},{24,8},{1,17},{9,25},{17,1},{25,9},{2,18},{10... | collective-permute-start | bytes 368648 | tf_op jit(solution)/shard_map/ppermute | solution.py:621
  32.6 5.9 %collective-permute-start.2 = (f32[240,128]{1,0:T(8,128)}, f32[240,128]{1,0:T(8,128)}, u32[]{:S(2)}, u32[]{:S(2)}) collective-permute-start(f32[240,128]{1,0:T(8,128)} %get-tuple-element.36), channel_id=1, source_target_pairs={{0,24},{8,16},{16,8},{24,0},{1,25},{9,17},{17,9},{25,1},{2,26},{10... | collective-permute-start | bytes 368648 | tf_op jit(solution)/shard_map/ppermute | solution.py:621
  32.6 5.9 %collective-permute-start = (f32[240,128]{1,0:T(8,128)}, f32[240,128]{1,0:T(8,128)}, u32[]{:S(2)}, u32[]{:S(2)}) collective-permute-start(f32[240,128]{1,0:T(8,128)} %get-tuple-element.36), channel_id=1, source_target_pairs={{0,8},{8,0},{16,24},{24,16},{1,9},{9,1},{17,25},{25,17},{2,10},{10... | collective-permute-start | bytes 368648 | tf_op jit(solution)/shard_map/ppermute | solution.py:621
  41.1 20.3 %all-to-all-start.2 = ((f32[8,120,128]{2,1,0:T(8,128)}), f32[8,120,128]{2,1,0:T(8,128)}, u32[]{:S(2)}, u32[]{:S(2)}) async-start(f32[8,120,128]{2,1,0:T(8,128)} %shard_map.70), calls=%async_computation.2 | async-start | bytes 983040 | tf_op jit(solution)/shard_map/all_to_all | solution.py:662
  61.4 2.2 %collective-permute-start.5 = (f32[8,120,128]{2,1,0:T(8,128)}, f32[8,120,128]{2,1,0:T(8,128)}, u32[]{:S(2)}, u32[]{:S(2)}) collective-permute-start(f32[8,120,128]{2,1,0:T(8,128)} %all-to-all-done.2.refs_2_), channel_id=1, source_target_pairs={{0,8},{8,0},{16,24},{24,16},{1,9},{9,1},{17,25},{25,17},{2,10},{10... | collective-permute-start | bytes 1474568 | tf_op jit(solution)/shard_map/ppermute | solution.py:681

commit v2 on v1

--- a/solution.py
+++ b/solution.py
@@ -254,7 +254,7 @@
                     to[pl.ds(row, 1), :] = got[2][sub[l] : sub[l] + 1]
             return 0
 
-        lax.fori_loop(0, CS, channel, 0, unroll=2)
+        lax.fori_loop(0, CS, channel, 0, unroll=3)
 
 
 def pick_band(z, anc, *refs):
@@ -468,7 +468,7 @@
                     back[x, pl.ds((l * C + c) * z.H + y, M, 3), :] = v
         return 0
 
-    lax.fori_loop(0, C, channel, 0, unroll=2)
+    lax.fori_loop(0, C, channel, 0, unroll=3)
     fine = iota((2 * z.W, z.W), 1)
     place = lax.rem(iota((2 * z.W, z.W), 0), z.W)
     at = lax.rem(place, LANES) * 3 + place // LANES
@@ -531,7 +531,7 @@
         out[c] = jnp.where(inside, share, step)
         return 0
 
-    lax.fori_loop(0, C, channel, 0, unroll=2)
+    lax.fori_loop(0, C, channel, 0, unroll=3)
 
 
 def both_steps(

time: 66.5 us -> 66.3 us (level)
  transfers between devices with their start and end apart: 9 -> 9, of which waited for: 5 -> 5; matrix products, arithmetic and copies ran while one was open for 0% -> 0% of each run, Pallas kernels for 35% -> 34%
where the time goes in v2:
time: 66.3 us; the launch traced here: 65.6 us
  Pallas kernels  29.9 us (45%)
  starting transfers between devices  25.7 us (39%)
  waiting for transfers between devices  9.28 us (14%)
  between operations  0.7 us (1%)
    pallas_call x5, Pallas kernels, call(): pl.pallas_call(kernel, out_shape=list(out_shape), in_specs=[place] * (n_i...  25.5 us
    all_to_all x1, starting transfers between devices, shards(): avg = lax.all_to_all(avg, 'dev', 0, 0, tiled=True)  6.72 us
    all_to_all x1, starting transfers between devices, shards(): ring = lax.all_to_all(ring, 'dev', 0, 0, tiled=True)  6.7 us
    ppermute x3, waiting for transfers between devices, shards(): lax.ppermute(x, 'grp', [(a, a ^ k) for a in range(z.G)])  5.35 us
    ppermute x1, starting transfers between devices, shards(): up = lax.ppermute(up, 'dev', forward)  4.62 us
    pallas_call x2, Pallas kernels, merge(): pl.pallas_call(kernel, out_shape=jax.ShapeDtypeStruct(base.shape, F32), i...  4.42 us
    all_to_all x1, starting transfers between devices, shards(): ring = lax.all_to_all(ring, 'grp', 0, 0, tiled=True)  4.22 us
    all_to_all x1, waiting for transfers between devices, shards(): avg = lax.all_to_all(avg, 'dev', 0, 0, tiled=True)  2.8 us
  transfers between devices with their start and end apart: 9, of which 5 were waited for; matrix products, arithmetic and copies ran while one was open for 0% of the time, Pallas kernels for 34%

profile of v2, /device:TPU:0, one launch (start us, length us, event | category | flops | bytes accessed | tf_op | source)
XLA Modules:
  0.0 65.6 jit_solution(17340579525795331372)
XLA Ops:
  0.6 3.4 %shard_map.68 = (f32[4,184,128]{2,1,0:T(8,128)}, f32[496,128]{1,0:T(8,128)}, f32[496,128]{1,0:T(8,128)}) custom-call(s32[2,8]{1,0:T(2,128)} %bitcast.1, f32[24,64,128]{2,1,0:T(8,128)} %refs_3_.1, f32[2,24,24,384]{3,2,1,0:T(8,128)} %refs_2_.3), custom_call_target="tpu_custom_call" | custom-call | tf_op jit(solution)/shard_map/pallas_call | solution.py:71
  4.0 4.2 %all-to-all-start = ((f32[4,184,128]{2,1,0:T(8,128)}), f32[4,184,128]{2,1,0:T(8,128)}, u32[]{:S(2)}, u32[]{:S(2)}) async-start(f32[4,184,128]{2,1,0:T(8,128)} %get-tuple-element.32), calls=%async_computation | async-start | bytes 753664 | tf_op jit(solution)/shard_map/all_to_all | solution.py:635
  8.2 6.9 %shard_map.69 = (f32[240,128]{1,0:T(8,128)}, f32[240,128]{1,0:T(8,128)}, f32[3,1152,128]{2,1,0:T(8,128)}) custom-call(f32[2,24]{1,0:T(2,128)} %refs_1_.5, f32[2,24]{1,0:T(2,128)} %refs_2_.4, f32[2,24,24,384]{3,2,1,0:T(8,128)} %refs_2_.3), custom_call_target="tpu_custom_call" | custom-call | tf_op jit(solution)/shard_map/pallas_call | solution.py:71
  15.1 0.9 %all-to-all-done.refs_0_ = f32[4,184,128]{2,1,0:T(8,128)} async-done(((f32[4,184,128]{2,1,0:T(8,128)}), f32[4,184,128]{2,1,0:T(8,128)}, u32[]{:S(2)}, u32[]{:S(2)}) %all-to-all-start) | async-done | bytes 376864 | tf_op jit(solution)/shard_map/all_to_all | solution.py:635
  16.0 1.9 %shard_map.71 = (f32[8,72,128]{2,1,0:T(8,128)}, f32[48,128]{1,0:T(8,128)}) custom-call(f32[4,184,128]{2,1,0:T(8,128)} %all-to-all-done.refs_0_), custom_call_target="tpu_custom_call" | custom-call | tf_op jit(solution)/shard_map/pallas_call | solution.py:71
  17.9 6.7 %all-to-all-start.1 = ((f32[8,72,128]{2,1,0:T(8,128)}), f32[8,72,128]{2,1,0:T(8,128)}, u32[]{:S(2)}, u32[]{:S(2)}) async-start(f32[8,72,128]{2,1,0:T(8,128)} %get-tuple-element.40), calls=%async_computation.1 | async-start | bytes 589824 | tf_op jit(solution)/shard_map/all_to_all | solution.py:657
  24.6 4.6 %collective-permute-start.3 = (f32[496,128]{1,0:T(8,128)}, f32[496,128]{1,0:T(8,128)}, u32[]{:S(2)}, u32[]{:S(2)}) collective-permute-start(f32[496,128]{1,0:T(8,128)} %get-tuple-element.41), channel_id=1, source_target_pairs={{0,1},{1,2},{2,3},{3,4},{4,5},{5,6},{6,7},{8,9},{9,10},{10,11},{11... | collective-permute-start | bytes 761864 | tf_op jit(solution)/shard_map/ppermute | solution.py:647
  29.2 1.3 %collective-permute-start.4 = (f32[496,128]{1,0:T(8,128)}, f32[496,128]{1,0:T(8,128)}, u32[]{:S(2)}, u32[]{:S(2)}) collective-permute-start(f32[496,128]{1,0:T(8,128)} %get-tuple-element.42), channel_id=1, source_target_pairs={{1,0},{2,1},{3,2},{4,3},{5,4},{6,5},{7,6},{9,8},{10,9},{11,10},{12... | collective-permute-start | bytes 761864 | tf_op jit(solution)/shard_map/ppermute | solution.py:648
  30.5 1.6 %collective-permute-start.1 = (f32[240,128]{1,0:T(8,128)}, f32[240,128]{1,0:T(8,128)}, u32[]{:S(2)}, u32[]{:S(2)}) collective-permute-start(f32[240,128]{1,0:T(8,128)} %get-tuple-element.35.refs_1_), channel_id=1, source_target_pairs={{0,16},{8,24},{16,0},{24,8},{1,17},{9,25},{17,1},{25,9},{2,18},{10... | collective-permute-start | bytes 368648 | tf_op jit(solution)/shard_map/ppermute | solution.py:621
  32.2 0.0 collective-permute-start.2
  32.2 0.6 collective-permute-start
  32.7 3.4 %collective-permute-done.1.refs_3_ = f32[240,128]{1,0:T(8,128)} collective-permute-done((f32[240,128]{1,0:T(8,128)}, f32[240,128]{1,0:T(8,128)}, u32[]{:S(2)}, u32[]{:S(2)}) %collective-permute-start.1) | collective-permute-done | bytes 122912 | tf_op jit(solution)/shard_map/ppermute | solution.py:621
  36.1 2.0 %collective-permute-done.2.refs_4_ = f32[240,128]{1,0:T(8,128)} collective-permute-done((f32[240,128]{1,0:T(8,128)}, f32[240,128]{1,0:T(8,128)}, u32[]{:S(2)}, u32[]{:S(2)}) %collective-permute-start.2) | collective-permute-done | bytes 122912 | tf_op jit(solution)/shard_map/ppermute | solution.py:621
  38.1 0.0 collective-permute-done.refs_2_
  38.1 2.2 %shard_map.70 = f32[8,120,128]{2,1,0:T(8,128)} custom-call(s32[2,8]{1,0:T(2,128)} %bitcast.2, f32[240,128]{1,0:T(8,128)} %get-tuple-element.35.refs_1_, f32[240,128]{1,0:T(8,128)} %collective-permute-done.refs_2_, f32[240,128]{1,0:T(8,128)} %collective-permute-done.1.refs_3_, f32[240,128]{1,0:T(8,128)} %collective-permute-done.2.refs_4_), custom_call_target="tpu_custom_call" | custom-call | tf_op jit(solution)/shard_map/pallas_call | solution.py:71
  40.3 0.2 collective-permute-done.3.refs_5_
  40.5 0.0 collective-permute-done.4.refs_6_
  40.5 0.0 all-to-all-done.1.refs_7_
  40.5 6.7 %all-to-all-start.2 = ((f32[8,120,128]{2,1,0:T(8,128)}), f32[8,120,128]{2,1,0:T(8,128)}, u32[]{:S(2)}, u32[]{:S(2)}) async-start(f32[8,120,128]{2,1,0:T(8,128)} %shard_map.70), calls=%async_computation.2 | async-start | bytes 983040 | tf_op jit(solution)/shard_map/all_to_all | solution.py:662
  47.2 11.1 %shard_map.72 = (f32[24,64,128]{2,1,0:T(8,128)}, f32[2,24,24,384]{3,2,1,0:T(8,128)}) custom-call(s32[2,8]{1,0:T(2,128)} %bitcast.3, f32[2,24]{1,0:T(2,128)} %refs_1_.5, f32[2,24]{1,0:T(2,128)} %refs_2_.4, f32[24,64,128]{2,1,0:T(8,128)} %refs_3_.1, f32[48,128]{1,0:T(8,128)} %get-tuple-element.44.refs_4_, f32[496,128]{1,0:T(8,128)} %collective-permute-done.3.refs_5_, ...), custom_call_target="tpu_custom_call" | custom-call | tf_op jit(solution)/shard_map/pallas_call | solution.py:71
  58.4 2.8 %all-to-all-done.2.refs_2_ = f32[8,120,128]{2,1,0:T(8,128)} async-done(((f32[8,120,128]{2,1,0:T(8,128)}), f32[8,120,128]{2,1,0:T(8,128)}, u32[]{:S(2)}, u32[]{:S(2)}) %all-to-all-start.2) | async-done | bytes 491552 | tf_op jit(solution)/shard_map/all_to_all | solution.py:662
  61.2 0.0 collective-permute-start.5
  61.2 2.2 %shard_map.73.refs_1_ = f32[24,64,128]{2,1,0:T(8,128)} custom-call(s32[2,8]{1,0:T(2,128)} %bitcast.4, f32[24,64,128]{2,1,0:T(8,128)} %get-tuple-element.51.refs_1_, f32[8,120,128]{2,1,0:T(8,128)} %all-to-all-done.2.refs_2_), custom_call_target="tpu_custom_call", output_to_operand_aliasing={{}: (1, {})} | custom-call | tf_op jit(solution)/shard_map/pallas_call | solution.py:599
  63.4 0.0 collective-permute-done.5.refs_2_
  63.4 2.2 %shard_map.74 = f32[24,64,128]{2,1,0:T(8,128)} custom-call(s32[2,8]{1,0:T(2,128)} %bitcast.5, f32[24,64,128]{2,1,0:T(8,128)} %shard_map.73.refs_1_, f32[8,120,128]{2,1,0:T(8,128)} %collective-permute-done.5.refs_2_), custom_call_target="tpu_custom_call", output_to_operand_aliasing={{}: (1, {})} | custom-call | tf_op jit(solution)/shard_map/pallas_call | solution.py:599
Async XLA Ops:
  4.0 12.1 %all-to-all-start = ((f32[4,184,128]{2,1,0:T(8,128)}), f32[4,184,128]{2,1,0:T(8,128)}, u32[]{:S(2)}, u32[]{:S(2)}) async-start(f32[4,184,128]{2,1,0:T(8,128)} %get-tuple-element.32), calls=%async_computation | async-start | bytes 753664 | tf_op jit(solution)/shard_map/all_to_all | solution.py:635
  17.9 22.6 %all-to-all-start.1 = ((f32[8,72,128]{2,1,0:T(8,128)}), f32[8,72,128]{2,1,0:T(8,128)}, u32[]{:S(2)}, u32[]{:S(2)}) async-start(f32[8,72,128]{2,1,0:T(8,128)} %get-tuple-element.40), calls=%async_computation.1 | async-start | bytes 589824 | tf_op jit(solution)/shard_map/all_to_all | solution.py:657
  24.6 15.9 %collective-permute-start.3 = (f32[496,128]{1,0:T(8,128)}, f32[496,128]{1,0:T(8,128)}, u32[]{:S(2)}, u32[]{:S(2)}) collective-permute-start(f32[496,128]{1,0:T(8,128)} %get-tuple-element.41), channel_id=1, source_target_pairs={{0,1},{1,2},{2,3},{3,4},{4,5},{5,6},{6,7},{8,9},{9,10},{10,11},{11... | collective-permute-start | bytes 761864 | tf_op jit(solution)/shard_map/ppermute | solution.py:647
  29.2 11.3 %collective-permute-start.4 = (f32[496,128]{1,0:T(8,128)}, f32[496,128]{1,0:T(8,128)}, u32[]{:S(2)}, u32[]{:S(2)}) collective-permute-start(f32[496,128]{1,0:T(8,128)} %get-tuple-element.42), channel_id=1, source_target_pairs={{1,0},{2,1},{3,2},{4,3},{5,4},{6,5},{7,6},{9,8},{10,9},{11,10},{12... | collective-permute-start | bytes 761864 | tf_op jit(solution)/shard_map/ppermute | solution.py:648
  30.5 5.6 %collective-permute-start.1 = (f32[240,128]{1,0:T(8,128)}, f32[240,128]{1,0:T(8,128)}, u32[]{:S(2)}, u32[]{:S(2)}) collective-permute-start(f32[240,128]{1,0:T(8,128)} %get-tuple-element.35.refs_1_), channel_id=1, source_target_pairs={{0,16},{8,24},{16,0},{24,8},{1,17},{9,25},{17,1},{25,9},{2,18},{10... | collective-permute-start | bytes 368648 | tf_op jit(solution)/shard_map/ppermute | solution.py:621
  32.2 5.9 %collective-permute-start.2 = (f32[240,128]{1,0:T(8,128)}, f32[240,128]{1,0:T(8,128)}, u32[]{:S(2)}, u32[]{:S(2)}) collective-permute-start(f32[240,128]{1,0:T(8,128)} %get-tuple-element.36), channel_id=1, source_target_pairs={{0,24},{8,16},{16,8},{24,0},{1,25},{9,17},{17,9},{25,1},{2,26},{10... | collective-permute-start | bytes 368648 | tf_op jit(solution)/shard_map/ppermute | solution.py:621
  32.2 5.9 %collective-permute-start = (f32[240,128]{1,0:T(8,128)}, f32[240,128]{1,0:T(8,128)}, u32[]{:S(2)}, u32[]{:S(2)}) collective-permute-start(f32[240,128]{1,0:T(8,128)} %get-tuple-element.36), channel_id=1, source_target_pairs={{0,8},{8,0},{16,24},{24,16},{1,9},{9,1},{17,25},{25,17},{2,10},{10... | collective-permute-start | bytes 368648 | tf_op jit(solution)/shard_map/ppermute | solution.py:621
  40.5 20.7 %all-to-all-start.2 = ((f32[8,120,128]{2,1,0:T(8,128)}), f32[8,120,128]{2,1,0:T(8,128)}, u32[]{:S(2)}, u32[]{:S(2)}) async-start(f32[8,120,128]{2,1,0:T(8,128)} %shard_map.70), calls=%async_computation.2 | async-start | bytes 983040 | tf_op jit(solution)/shard_map/all_to_all | solution.py:662
  61.2 2.2 %collective-permute-start.5 = (f32[8,120,128]{2,1,0:T(8,128)}, f32[8,120,128]{2,1,0:T(8,128)}, u32[]{:S(2)}, u32[]{:S(2)}) collective-permute-start(f32[8,120,128]{2,1,0:T(8,128)} %all-to-all-done.2.refs_2_), channel_id=1, source_target_pairs={{0,8},{8,0},{16,24},{24,16},{1,9},{9,1},{17,25},{25,17},{2,10},{10... | collective-permute-start | bytes 1474568 | tf_op jit(solution)/shard_map/ppermute | solution.py:681

commit v3 on v2

--- a/solution.py
+++ b/solution.py
@@ -101,6 +101,14 @@
     return found
 
 
+def deal_table(z, fine_dim):
+    fine = iota((z.W, z.W), fine_dim)
+    place = iota((z.W, z.W), 1 - fine_dim)
+    at = jnp.bitwise_and(place, LANES - 1) * 3 + jnp.right_shift(place, 7)
+    once = jnp.where(fine == at, 1.0, 0.0).astype(BF16)
+    return jnp.concatenate([once, once], axis=0)
+
+
 def weights(diff, cour, c, times):
     splat = lambda ref, k: jnp.full((8, LANES), ref[k, c], F32)
     east = times * splat(diff, 0)
@@ -206,10 +214,7 @@
     d = lax.axis_index("dev")
     own = lax.rem(lax.axis_index("grp"), z.S)
     C, M, CS = z.C, z.M, z.CS
-    fine = lax.rem(iota((2 * z.W, z.W), 0), z.W)
-    place = iota((2 * z.W, z.W), 1)
-    at = lax.rem(place, LANES) * 3 + place // LANES
-    deal = jnp.where(fine == at, 1.0, 0.0).astype(BF16)
+    deal = deal_table(z, 0)
     rows = C * z.H
     for l in range(z.L):
         fetch[l].wait()
@@ -401,9 +406,7 @@
     d = lax.axis_index("dev")
     C, M = z.C, z.M
     strip = Strip()
-    fine = lax.rem(iota((2 * z.W, z.W), 0), z.W)
-    place = iota((2 * z.W, z.W), 1)
-    deal = jnp.where(fine == lax.rem(place, LANES) * 3 + place // LANES, 1.0, 0.0).astype(BF16)
+    deal = deal_table(z, 0)
     for source, target in ((up_in, up), (dn_in, dn)):
         halo = [source[x * z.HALO : (x + 1) * z.HALO, :] for x in range(3)]
         dealt = split_dot(jnp.concatenate(halo, axis=1), deal)
@@ -469,10 +472,7 @@
         return 0
 
     lax.fori_loop(0, C, channel, 0, unroll=3)
-    fine = iota((2 * z.W, z.W), 1)
-    place = lax.rem(iota((2 * z.W, z.W), 0), z.W)
-    at = lax.rem(place, LANES) * 3 + place // LANES
-    undeal = jnp.where(fine == at, 1.0, 0.0).astype(BF16)
+    undeal = deal_table(z, 1)
     done = split_dot(jnp.concatenate([back[0], back[1], back[2]], axis=1), undeal)
     out[...] = done.reshape(z.L, C, z.H, z.W)
 

time: 66.3 us -> 66.3 us (level)
  no operation moved by 1% of the time
where the time goes in v3:
time: 66.3 us; the launch traced here: 65.6 us
  Pallas kernels  29.8 us (45%)
  starting transfers between devices  25.8 us (39%)
  waiting for transfers between devices  9.37 us (14%)
  between operations  0.7 us (1%)
    pallas_call x5, Pallas kernels, call(): pl.pallas_call(kernel, out_shape=list(out_shape), in_specs=[place] * (n_i...  25.4 us
    all_to_all x1, starting transfers between devices, shards(): avg = lax.all_to_all(avg, 'dev', 0, 0, tiled=True)  6.72 us
    all_to_all x1, starting transfers between devices, shards(): ring = lax.all_to_all(ring, 'dev', 0, 0, tiled=True)  6.7 us
    ppermute x3, waiting for transfers between devices, shards(): lax.ppermute(x, 'grp', [(a, a ^ k) for a in range(z.G)])  5.36 us
    ppermute x1, starting transfers between devices, shards(): up = lax.ppermute(up, 'dev', forward)  4.62 us
    pallas_call x2, Pallas kernels, merge(): pl.pallas_call(kernel, out_shape=jax.ShapeDtypeStruct(base.shape, F32), i...  4.42 us
    all_to_all x1, starting transfers between devices, shards(): ring = lax.all_to_all(ring, 'grp', 0, 0, tiled=True)  4.22 us
    all_to_all x1, waiting for transfers between devices, shards(): avg = lax.all_to_all(avg, 'dev', 0, 0, tiled=True)  2.91 us
  transfers between devices with their start and end apart: 9, of which 5 were waited for; matrix products, arithmetic and copies ran while one was open for 0% of the time, Pallas kernels for 34%

profile of v3, /device:TPU:0, one launch (start us, length us, event | category | flops | bytes accessed | tf_op | source)
XLA Modules:
  0.0 65.6 jit_solution(12381999573765200437)
XLA Ops:
  0.6 3.4 %shard_map.68 = (f32[4,184,128]{2,1,0:T(8,128)}, f32[496,128]{1,0:T(8,128)}, f32[496,128]{1,0:T(8,128)}) custom-call(s32[2,8]{1,0:T(2,128)} %bitcast.1, f32[24,64,128]{2,1,0:T(8,128)} %refs_3_.1, f32[2,24,24,384]{3,2,1,0:T(8,128)} %refs_2_.3), custom_call_target="tpu_custom_call" | custom-call | tf_op jit(solution)/shard_map/pallas_call | solution.py:71
  4.0 4.2 %all-to-all-start = ((f32[4,184,128]{2,1,0:T(8,128)}), f32[4,184,128]{2,1,0:T(8,128)}, u32[]{:S(2)}, u32[]{:S(2)}) async-start(f32[4,184,128]{2,1,0:T(8,128)} %get-tuple-element.32), calls=%async_computation | async-start | bytes 753664 | tf_op jit(solution)/shard_map/all_to_all | solution.py:635
  8.2 6.9 %shard_map.69 = (f32[240,128]{1,0:T(8,128)}, f32[240,128]{1,0:T(8,128)}, f32[3,1152,128]{2,1,0:T(8,128)}) custom-call(f32[2,24]{1,0:T(2,128)} %refs_1_.5, f32[2,24]{1,0:T(2,128)} %refs_2_.4, f32[2,24,24,384]{3,2,1,0:T(8,128)} %refs_2_.3), custom_call_target="tpu_custom_call" | custom-call | tf_op jit(solution)/shard_map/pallas_call | solution.py:71
  15.1 0.9 %all-to-all-done.refs_0_ = f32[4,184,128]{2,1,0:T(8,128)} async-done(((f32[4,184,128]{2,1,0:T(8,128)}), f32[4,184,128]{2,1,0:T(8,128)}, u32[]{:S(2)}, u32[]{:S(2)}) %all-to-all-start) | async-done | bytes 376864 | tf_op jit(solution)/shard_map/all_to_all | solution.py:635
  16.0 1.9 %shard_map.71 = (f32[8,72,128]{2,1,0:T(8,128)}, f32[48,128]{1,0:T(8,128)}) custom-call(f32[4,184,128]{2,1,0:T(8,128)} %all-to-all-done.refs_0_), custom_call_target="tpu_custom_call" | custom-call | tf_op jit(solution)/shard_map/pallas_call | solution.py:71
  17.9 6.7 %all-to-all-start.1 = ((f32[8,72,128]{2,1,0:T(8,128)}), f32[8,72,128]{2,1,0:T(8,128)}, u32[]{:S(2)}, u32[]{:S(2)}) async-start(f32[8,72,128]{2,1,0:T(8,128)} %get-tuple-element.40), calls=%async_computation.1 | async-start | bytes 589824 | tf_op jit(solution)/shard_map/all_to_all | solution.py:657
  24.6 4.6 %collective-permute-start.3 = (f32[496,128]{1,0:T(8,128)}, f32[496,128]{1,0:T(8,128)}, u32[]{:S(2)}, u32[]{:S(2)}) collective-permute-start(f32[496,128]{1,0:T(8,128)} %get-tuple-element.41), channel_id=1, source_target_pairs={{0,1},{1,2},{2,3},{3,4},{4,5},{5,6},{6,7},{8,9},{9,10},{10,11},{11... | collective-permute-start | bytes 761864 | tf_op jit(solution)/shard_map/ppermute | solution.py:647
  29.2 1.3 %collective-permute-start.4 = (f32[496,128]{1,0:T(8,128)}, f32[496,128]{1,0:T(8,128)}, u32[]{:S(2)}, u32[]{:S(2)}) collective-permute-start(f32[496,128]{1,0:T(8,128)} %get-tuple-element.42), channel_id=1, source_target_pairs={{1,0},{2,1},{3,2},{4,3},{5,4},{6,5},{7,6},{9,8},{10,9},{11,10},{12... | collective-permute-start | bytes 761864 | tf_op jit(solution)/shard_map/ppermute | solution.py:648
  30.5 1.6 %collective-permute-start.1 = (f32[240,128]{1,0:T(8,128)}, f32[240,128]{1,0:T(8,128)}, u32[]{:S(2)}, u32[]{:S(2)}) collective-permute-start(f32[240,128]{1,0:T(8,128)} %get-tuple-element.35.refs_1_), channel_id=1, source_target_pairs={{0,16},{8,24},{16,0},{24,8},{1,17},{9,25},{17,1},{25,9},{2,18},{10... | collective-permute-start | bytes 368648 | tf_op jit(solution)/shard_map/ppermute | solution.py:621
  32.2 0.0 collective-permute-start.2
  32.2 0.6 collective-permute-start
  32.7 3.4 %collective-permute-done.1.refs_3_ = f32[240,128]{1,0:T(8,128)} collective-permute-done((f32[240,128]{1,0:T(8,128)}, f32[240,128]{1,0:T(8,128)}, u32[]{:S(2)}, u32[]{:S(2)}) %collective-permute-start.1) | collective-permute-done | bytes 122912 | tf_op jit(solution)/shard_map/ppermute | solution.py:621
  36.1 2.0 %collective-permute-done.2.refs_4_ = f32[240,128]{1,0:T(8,128)} collective-permute-done((f32[240,128]{1,0:T(8,128)}, f32[240,128]{1,0:T(8,128)}, u32[]{:S(2)}, u32[]{:S(2)}) %collective-permute-start.2) | collective-permute-done | bytes 122912 | tf_op jit(solution)/shard_map/ppermute | solution.py:621
  38.1 0.0 collective-permute-done.refs_2_
  38.1 2.3 %shard_map.70 = f32[8,120,128]{2,1,0:T(8,128)} custom-call(s32[2,8]{1,0:T(2,128)} %bitcast.2, f32[240,128]{1,0:T(8,128)} %get-tuple-element.35.refs_1_, f32[240,128]{1,0:T(8,128)} %collective-permute-done.refs_2_, f32[240,128]{1,0:T(8,128)} %collective-permute-done.1.refs_3_, f32[240,128]{1,0:T(8,128)} %collective-permute-done.2.refs_4_), custom_call_target="tpu_custom_call" | custom-call | tf_op jit(solution)/shard_map/pallas_call | solution.py:71
  40.4 0.2 collective-permute-done.3.refs_5_
  40.5 0.0 collective-permute-done.4.refs_6_
  40.5 0.0 all-to-all-done.1.refs_7_
  40.5 6.7 %all-to-all-start.2 = ((f32[8,120,128]{2,1,0:T(8,128)}), f32[8,120,128]{2,1,0:T(8,128)}, u32[]{:S(2)}, u32[]{:S(2)}) async-start(f32[8,120,128]{2,1,0:T(8,128)} %shard_map.70), calls=%async_computation.2 | async-start | bytes 983040 | tf_op jit(solution)/shard_map/all_to_all | solution.py:662
  47.3 11.0 %shard_map.72 = (f32[24,64,128]{2,1,0:T(8,128)}, f32[2,24,24,384]{3,2,1,0:T(8,128)}) custom-call(s32[2,8]{1,0:T(2,128)} %bitcast.3, f32[2,24]{1,0:T(2,128)} %refs_1_.5, f32[2,24]{1,0:T(2,128)} %refs_2_.4, f32[24,64,128]{2,1,0:T(8,128)} %refs_3_.1, f32[48,128]{1,0:T(8,128)} %get-tuple-element.44.refs_4_, f32[496,128]{1,0:T(8,128)} %collective-permute-done.3.refs_5_, ...), custom_call_target="tpu_custom_call" | custom-call | tf_op jit(solution)/shard_map/pallas_call | solution.py:71
  58.3 2.9 %all-to-all-done.2.refs_2_ = f32[8,120,128]{2,1,0:T(8,128)} async-done(((f32[8,120,128]{2,1,0:T(8,128)}), f32[8,120,128]{2,1,0:T(8,128)}, u32[]{:S(2)}, u32[]{:S(2)}) %all-to-all-start.2) | async-done | bytes 491552 | tf_op jit(solution)/shard_map/all_to_all | solution.py:662
  61.2 0.0 collective-permute-start.5
  61.2 2.2 %shard_map.73.refs_1_ = f32[24,64,128]{2,1,0:T(8,128)} custom-call(s32[2,8]{1,0:T(2,128)} %bitcast.4, f32[24,64,128]{2,1,0:T(8,128)} %get-tuple-element.51.refs_1_, f32[8,120,128]{2,1,0:T(8,128)} %all-to-all-done.2.refs_2_), custom_call_target="tpu_custom_call", output_to_operand_aliasing={{}: (1, {})} | custom-call | tf_op jit(solution)/shard_map/pallas_call | solution.py:599
  63.4 0.0 collective-permute-done.5.refs_2_
  63.4 2.2 %shard_map.74 = f32[24,64,128]{2,1,0:T(8,128)} custom-call(s32[2,8]{1,0:T(2,128)} %bitcast.5, f32[24,64,128]{2,1,0:T(8,128)} %shard_map.73.refs_1_, f32[8,120,128]{2,1,0:T(8,128)} %collective-permute-done.5.refs_2_), custom_call_target="tpu_custom_call", output_to_operand_aliasing={{}: (1, {})} | custom-call | tf_op jit(solution)/shard_map/pallas_call | solution.py:599
Async XLA Ops:
  4.0 12.1 %all-to-all-start = ((f32[4,184,128]{2,1,0:T(8,128)}), f32[4,184,128]{2,1,0:T(8,128)}, u32[]{:S(2)}, u32[]{:S(2)}) async-start(f32[4,184,128]{2,1,0:T(8,128)} %get-tuple-element.32), calls=%async_computation | async-start | bytes 753664 | tf_op jit(solution)/shard_map/all_to_all | solution.py:635
  17.9 22.6 %all-to-all-start.1 = ((f32[8,72,128]{2,1,0:T(8,128)}), f32[8,72,128]{2,1,0:T(8,128)}, u32[]{:S(2)}, u32[]{:S(2)}) async-start(f32[8,72,128]{2,1,0:T(8,128)} %get-tuple-element.40), calls=%async_computation.1 | async-start | bytes 589824 | tf_op jit(solution)/shard_map/all_to_all | solution.py:657
  24.6 15.9 %collective-permute-start.3 = (f32[496,128]{1,0:T(8,128)}, f32[496,128]{1,0:T(8,128)}, u32[]{:S(2)}, u32[]{:S(2)}) collective-permute-start(f32[496,128]{1,0:T(8,128)} %get-tuple-element.41), channel_id=1, source_target_pairs={{0,1},{1,2},{2,3},{3,4},{4,5},{5,6},{6,7},{8,9},{9,10},{10,11},{11... | collective-permute-start | bytes 761864 | tf_op jit(solution)/shard_map/ppermute | solution.py:647
  29.2 11.3 %collective-permute-start.4 = (f32[496,128]{1,0:T(8,128)}, f32[496,128]{1,0:T(8,128)}, u32[]{:S(2)}, u32[]{:S(2)}) collective-permute-start(f32[496,128]{1,0:T(8,128)} %get-tuple-element.42), channel_id=1, source_target_pairs={{1,0},{2,1},{3,2},{4,3},{5,4},{6,5},{7,6},{9,8},{10,9},{11,10},{12... | collective-permute-start | bytes 761864 | tf_op jit(solution)/shard_map/ppermute | solution.py:648
  30.5 5.6 %collective-permute-start.1 = (f32[240,128]{1,0:T(8,128)}, f32[240,128]{1,0:T(8,128)}, u32[]{:S(2)}, u32[]{:S(2)}) collective-permute-start(f32[240,128]{1,0:T(8,128)} %get-tuple-element.35.refs_1_), channel_id=1, source_target_pairs={{0,16},{8,24},{16,0},{24,8},{1,17},{9,25},{17,1},{25,9},{2,18},{10... | collective-permute-start | bytes 368648 | tf_op jit(solution)/shard_map/ppermute | solution.py:621
  32.2 5.9 %collective-permute-start.2 = (f32[240,128]{1,0:T(8,128)}, f32[240,128]{1,0:T(8,128)}, u32[]{:S(2)}, u32[]{:S(2)}) collective-permute-start(f32[240,128]{1,0:T(8,128)} %get-tuple-element.36), channel_id=1, source_target_pairs={{0,24},{8,16},{16,8},{24,0},{1,25},{9,17},{17,9},{25,1},{2,26},{10... | collective-permute-start | bytes 368648 | tf_op jit(solution)/shard_map/ppermute | solution.py:621
  32.2 5.9 %collective-permute-start = (f32[240,128]{1,0:T(8,128)}, f32[240,128]{1,0:T(8,128)}, u32[]{:S(2)}, u32[]{:S(2)}) collective-permute-start(f32[240,128]{1,0:T(8,128)} %get-tuple-element.36), channel_id=1, source_target_pairs={{0,8},{8,0},{16,24},{24,16},{1,9},{9,1},{17,25},{25,17},{2,10},{10... | collective-permute-start | bytes 368648 | tf_op jit(solution)/shard_map/ppermute | solution.py:621
  40.5 20.7 %all-to-all-start.2 = ((f32[8,120,128]{2,1,0:T(8,128)}), f32[8,120,128]{2,1,0:T(8,128)}, u32[]{:S(2)}, u32[]{:S(2)}) async-start(f32[8,120,128]{2,1,0:T(8,128)} %shard_map.70), calls=%async_computation.2 | async-start | bytes 983040 | tf_op jit(solution)/shard_map/all_to_all | solution.py:662
  61.2 2.2 %collective-permute-start.5 = (f32[8,120,128]{2,1,0:T(8,128)}, f32[8,120,128]{2,1,0:T(8,128)}, u32[]{:S(2)}, u32[]{:S(2)}) collective-permute-start(f32[8,120,128]{2,1,0:T(8,128)} %all-to-all-done.2.refs_2_), channel_id=1, source_target_pairs={{0,8},{8,0},{16,24},{24,16},{1,9},{9,1},{17,25},{25,17},{2,10},{10... | collective-permute-start | bytes 1474568 | tf_op jit(solution)/shard_map/ppermute | solution.py:681
